TPU v7x, 32 devices: a whole 2x2x4 slice. The times are simulated.
32 devices in a mesh: row: 4 (over y, x), col: 8 (over z, core).
Axes of the slice: x: 2, y: 2, z: 4, core: 2. Of those that a mesh axis runs over, the one named last changes fastest.
Arguments:
- doubles: float32 [32, 32, 192, 192], P(None, None, 'row', 'col'), may hold values from -6 to 6
- cycle_inter: float32 [6144, 6144], P('row', 'col'), may hold values from -0.078125 to 0.078125
Outputs:
- cycle_term: float32 [6144, 6144], P('row', 'col')
All inputs are finite; a program needn't handle non-finite values.
Results may differ from a plain program's by a relative error of at most 0.00007.
Values sent between devices are 32-bit elements; how exact they have to be, the bound alone decides.
No kernel may reach another device: no remote copies, remote signals or barrier semaphores. Data moves between devices by JAX's collectives and lax.ppermute only.
A program may use at most 192 MiB of HBM per device.

v0:
```python
import jax
import jax.numpy as jnp
from jax import lax
from jax.sharding import PartitionSpec as P

V = 192


def body(doubles, cycle_inter):
    moved = lax.all_to_all(
        lax.all_to_all(doubles, "row", split_axis=0, concat_axis=2, tiled=True),
        "col",
        split_axis=1,
        concat_axis=3,
        tiled=True,
    )
    kloc = moved.shape[0]
    jloc = moved.shape[1]
    local_panel = jnp.transpose(moved, (0, 2, 1, 3)).reshape(kloc * V, jloc * V)
    amp_panel = lax.all_gather(local_panel, "row", axis=0, tiled=True)
    return jnp.dot(
        lax.all_gather(cycle_inter, "col", axis=1, tiled=True),
        amp_panel,
        precision=lax.Precision.HIGHEST,
        preferred_element_type=jnp.float32,
    )


def solution(mesh):
    placed = (P(None, None, "row", "col"), P("row", "col"))
    return jax.shard_map(
        body, mesh=mesh, in_specs=placed, out_specs=P("row", "col"), check_vma=False
    )
```

profile of v0, /device:TPU:0, one launch (start us, length us, event | category | flops | bytes accessed | tf_op | source)
XLA Modules:
  0.0 910.1 jit_solution(12585892719018246135)
XLA Ops:
  6.5 0.0 all-gather.5.cloned.1.call-start
  6.5 15.0 %reshape.4 = f32[4,1,294912]{2,1,0:T(1,128)} reshape(f32[32,32,24,48]{3,2,1,0:T(8,128)} %bitcast.24) | data formatting | bytes 9437184
  21.5 61.2 %all_to_all.36 = f32[4,1,294912]{2,1,0:T(1,128)} all-to-all(f32[4,1,294912]{2,1,0:T(1,128)} %reshape.4), channel_id=1, replica_groups=mesh['row'=4,'col'=8] {'row'}, dimensions={0} | all-to-all | bytes 9437184 | tf_op jit(solution)/shard_map/all_to_all | solution.py:11
  82.7 0.6 broadcast
  83.3 16.9 %reduce = f32[4,294912]{1,0:T(4,128)} reduce(f32[4,1,294912]{2,1,0:T(1,128)} %all_to_all.36, f32[]{:T(128)} %broadcast), dimensions={1}, to_apply=%all_to_all.26.reduce_sub_computation | reduce | bytes 9437188 | tf_op jit(solution)/shard_map/all_to_all | solution.py:11
  100.1 12.6 %reshape.5 = f32[32,32,24,48]{3,2,1,0:T(8,128)} reshape(f32[4,294912]{1,0:T(4,128)} %reduce) | data formatting | bytes 9437184
  112.7 16.5 %copy.16 = f32[4,8,32,48,24]{3,0,4,2,1:T(4,128)} copy(f32[4,8,32,48,24]{3,4,2,1,0:T(8,128)} %bitcast.20) | data formatting | bytes 9437184 | tf_op jit(solution)/shard_map/all_to_all | solution.py:11
  129.3 11.9 %all_to_all.29 = f32[8,32,192,24]{2,3,1,0:T(8,128)} reshape(f32[8,32,4,48,24]{3,2,4,1,0:T(4,128)} %bitcast.21) | data formatting | bytes 9437184 | tf_op jit(solution)/shard_map/all_to_all | solution.py:11
  141.2 3.6 copy.10
  144.8 143.8 %all_to_all.37 = f32[8,32,192,24]{2,3,0,1:T(8,128)S(1)} all-to-all(f32[8,32,192,24]{2,3,0,1:T(8,128)S(1)} %copy.10), channel_id=1, replica_groups=mesh['row'=4,'col'=8] {'col'}, dimensions={1} | all-to-all | bytes 9437184 | tf_op jit(solution)/shard_map/all_to_all | solution.py:10
  288.6 0.8 copy.12
  289.4 6.3 copy.13
  295.7 7.4 reshape.3
  303.2 0.0 all-gather.5.cloned.1.call-update
  303.2 0.0 all-gather.3.cloned.1.call-start
  303.2 0.7 all-gather.3.cloned.1.call-update
  303.9 172.6 %all-gather.5.cloned.1.call-done = f32[6144,768]{0,1:T(8,128)} async-done(((f32[1536,768]{0,1:T(8,128)}), f32[6144,768]{0,1:T(8,128)}) %all-gather.5.cloned.1.call-update) | async-done | bytes 18874384 | tf_op jit(solution)/shard_map/all_gather | solution.py:20
  476.5 326.2 %all-gather.3.cloned.1.call-done = f32[1536,6144]{1,0:T(8,128)} async-done(((f32[1536,768]{1,0:T(8,128)}), f32[1536,6144]{1,0:T(8,128)}) %all-gather.3.cloned.1.call-update) | async-done | bytes 37748752 | tf_op jit(solution)/shard_map/all_gather | solution.py:22
  802.7 100.6 %fusion = f32[1536,768]{1,0:T(8,128)} fusion(f32[1536,6144]{1,0:T(8,128)} %all-gather.3.cloned.1.call-done, f32[6144,768]{0,1:T(8,128)} %all-gather.5.cloned.1.call-done), kind=kOutput, calls=%fused_computation.1 | convolution fusion | flops 86973087744 | bytes 61341696 | tf_op jit(solution)/shard_map/dot_general | solution.py:21
Async XLA Ops:
  6.5 470.0 %all-gather.5.cloned.1.call-start = ((), (), s32[]{:S(2)}) async-start(), calls=%async_computation.3 | async-start | bytes 23592960 | tf_op jit(solution)/shard_map/all_gather | solution.py:20
  303.2 499.5 %all-gather.3.cloned.1.call-start = ((), (), s32[]{:S(2)}) async-start(), calls=%async_computation.2 | async-start | bytes 42467328 | tf_op jit(solution)/shard_map/all_gather | solution.py:22
Sparse Core Ops, SparseCore 0:
  303.3 173.1 all-gather.4
  478.1 324.5 all-gather.2
where the time goes:
time: 911 us; the launch traced here: 910 us
  waiting for transfers between devices  499 us (55%)
  blocking collectives  205 us (23%)
  matrix products  101 us (11%)
  local copies, waits for them, and re-layouts  74.8 us (8%)
  other arithmetic  16.9 us (2%)
  between operations  13.4 us (1%)
    all_gather x1, waiting for transfers between devices, body(): lax.all_gather(cycle_inter, 'col', axis=1, tiled=True)  326 us
    all_gather x1, waiting for transfers between devices, body(): amp_panel = lax.all_gather(local_panel, 'row', axis=0, tiled=True)  173 us
    all_to_all x1, blocking collectives, body(): lax.all_to_all(lax.all_to_all(doubles, 'row', split_axis=0, concat_axis=2...  144 us
    dot_general x1, matrix products, body(): jnp.dot(lax.all_gather(cycle_inter, 'col', axis=1, tiled=True), amp_panel...  101 us
    all_to_all x1, blocking collectives, body(): lax.all_to_all(doubles, 'row', split_axis=0, concat_axis=2, tiled=True)  61.2 us
    all_to_all x4, local copies, waits for them, and re-layouts, body(): lax.all_to_all(doubles, 'row', split_axis=0, concat_axis=2, tiled=True)  32.6 us
    unnamed x2, local copies, waits for them, and re-layouts  27.6 us
  transfers between devices with their start and end apart: 2, of which 2 were waited for; matrix products, arithmetic and copies ran while one was open for 0% of the time, Pallas kernels for 0%

commit v1 on v0

v1 whole, which is shorter than its diff:
```python
import functools

import jax
import jax.numpy as jnp
from jax import lax
from jax.experimental import pallas as pl
from jax.experimental.pallas import tpu as pltpu
from jax.sharding import PartitionSpec as P


NT = (((1,), (1,)), ((), ()))


def params(mib):
    return pltpu.CompilerParams(vmem_limit_bytes=mib * 2**20)


def cost(flops, moved):
    return pl.CostEstimate(flops=flops, bytes_accessed=moved, transcendentals=0)


def after(x, *deps):
    return lax.optimization_barrier((x,) + deps)[0]


def pack(blocks, t, planes, received=None):
    k, j, vb, vr = t.shape
    jl = j // (2 * planes)
    rows, lanes = jl * vb, k * vr

    def fill(t_ref, put):
        for jj in range(jl):
            put(
                slice(jj * vb, (jj + 1) * vb),
                jnp.concatenate([t_ref[kk, jj] for kk in range(k)], axis=-1),
            )

    def give(blocks_ref, t_ref, o_ref):
        def put(at, x):
            o_ref[0, at] = x

        fill(t_ref, put)

    def merge(blocks_ref, t_ref, got_ref, *outs):
        for d in range(planes):

            @pl.when(pl.program_id(0) == d)
            def _():
                def put(at, x):
                    outs[d][0, at] = x

                fill(t_ref, put)
                outs[d][1] = got_ref[0]

    t_spec = pl.BlockSpec((k, jl, vb, vr), lambda i, b: (0, b[i], 0, 0))
    given = pl.BlockSpec((1, rows, lanes), lambda i, b: (i, 0, 0))
    if received is None:
        kernel, args, ins, outs = give, (), [t_spec], given
        shape = jax.ShapeDtypeStruct((planes, rows, lanes), t.dtype)
    else:
        kernel, args, ins = merge, (received,), [t_spec, given]
        outs = [pl.BlockSpec((2, rows, lanes), lambda i, b: (0, 0, 0))] * planes
        shape = [jax.ShapeDtypeStruct((2, rows, lanes), t.dtype)] * planes
    return pl.pallas_call(
        kernel,
        grid_spec=pltpu.PrefetchScalarGridSpec(
            num_scalar_prefetch=1, grid=(planes,), in_specs=ins, out_specs=outs
        ),
        out_shape=shape,
        compiler_params=params(40),
        cost_estimate=cost(0, 5 * t.size),
    )(blocks, t, *args)


def panel(where, came, planes, vb, kp, vr):
    rows_r = len(came)
    rows, lanes = came[0][0][0].shape[1:]
    jl = rows // vb
    lw = kp * vr
    vcol = 2 * planes * vb
    arrays = [x for e in came for d in e for x in d]
    index = []
    for e in range(rows_r):
        for d in range(planes):
            index += [
                (e, d, n, first)
                for n, x in enumerate(arrays)
                if any(x is y for y in came[e][d])
                for first in range(x.shape[0])
            ]

    def kernel(w_ref, *refs):
        hi_ref, lo_ref, x_ref = refs[len(arrays) :]
        p, core, r = w_ref[0], w_ref[1], w_ref[2]
        seen = {}
        for e, d, n, first in index:
            c = seen.get((e, d), 0)
            seen[e, d] = c + 1
            src = (p ^ d) * 2 + (core ^ c)
            to = pl.multiple_of(src * vb, vb)
            x_ref[r ^ e, pl.ds(to, vb)] = refs[n][first]
        for k in range(0, kp, 2):
            x = jnp.concatenate(
                [
                    x_ref[q, :, (k + kk) * vr : (k + kk + 1) * vr]
                    for kk in range(2)
                    for q in range(rows_r)
                ],
                axis=-1,
            )
            at = slice(k * rows_r * vr, (k + 2) * rows_r * vr)
            hi = x.astype(jnp.bfloat16)
            hi_ref[:, at] = hi
            lo_ref[:, at] = (x - hi.astype(jnp.float32)).astype(jnp.bfloat16)

    out = pl.BlockSpec((vcol, rows_r * lw), lambda t, j, w: (j, t))
    shape = jax.ShapeDtypeStruct((jl * vcol, rows_r * lanes), jnp.bfloat16)
    return pl.pallas_call(
        kernel,
        grid_spec=pltpu.PrefetchScalarGridSpec(
            num_scalar_prefetch=1,
            grid=(lanes // lw, jl),
            in_specs=[
                pl.BlockSpec((x.shape[0], vb, lw), lambda t, j, w: (0, j, t))
                for x in arrays
            ],
            out_specs=[out, out],
            scratch_shapes=[pltpu.VMEM((rows_r, vcol, lw), jnp.float32)],
        ),
        out_shape=[shape, shape],
        compiler_params=params(40),
        cost_estimate=cost(0, 8 * jl * vcol * rows_r * lanes),
    )(where, *arrays)


def product(a, hilo, into, start, rows):
    hi, lo = hilo
    n, depth = hi.shape
    m = a.shape[0]
    tk = depth // 8

    def kernel(a_ref, h_ref, l_ref, *refs):
        o_ref, x_ref = refs[-2:]

        @pl.when(pl.program_id(0) == 0)
        def _():
            o_ref[...] = jnp.zeros_like(o_ref)

        dot = functools.partial(
            lax.dot_general, dimension_numbers=NT, preferred_element_type=jnp.float32
        )
        x = a_ref[...]
        xh = x.astype(jnp.bfloat16)
        x_ref[:m] = xh
        x_ref[m:] = (x - xh.astype(jnp.float32)).astype(jnp.bfloat16)
        both = dot(x_ref[...], h_ref[...])
        o_ref[...] += both[:m] + both[m:] + dot(x_ref[:m], l_ref[...])

    specs = [pl.BlockSpec((m, tk), lambda i: (0, i))]
    specs += [pl.BlockSpec((n, tk), lambda i: (0, i))] * 2
    args, alias = [a, hi, lo], {}
    if into is not None:
        args.append(into)
        specs.append(pl.BlockSpec(memory_space=pl.ANY))
        alias = {3: 0}
    return pl.pallas_call(
        kernel,
        grid=(depth // tk,),
        in_specs=specs,
        out_specs=pl.BlockSpec((m, n), lambda i: (start // m, 0)),
        out_shape=jax.ShapeDtypeStruct((rows, n), jnp.float32),
        scratch_shapes=[pltpu.VMEM((2 * m, tk), jnp.bfloat16)],
        input_output_aliases=alias,
        compiler_params=params(52),
        cost_estimate=cost(6 * m * n * depth, 4 * m * depth + 4 * n * depth),
    )(*args)


def plain(doubles, cycle_inter):
    vs = doubles.shape[2] * lax.axis_size("row")
    moved = lax.all_to_all(
        lax.all_to_all(doubles, "row", split_axis=0, concat_axis=2, tiled=True),
        "col",
        split_axis=1,
        concat_axis=3,
        tiled=True,
    )
    local_panel = jnp.transpose(moved, (0, 2, 1, 3)).reshape(moved.shape[0] * vs, -1)
    amp_panel = lax.all_gather(local_panel, "row", axis=0, tiled=True)
    return jnp.dot(
        lax.all_gather(cycle_inter, "col", axis=1, tiled=True),
        amp_panel,
        precision=lax.Precision.HIGHEST,
        preferred_element_type=jnp.float32,
    )


def line(doubles, cycle_inter, rows_r, planes):
    k, j, vr, vb = doubles.shape
    col, r = lax.axis_index("col"), lax.axis_index("row")
    p, core = col // 2, col % 2
    where = jnp.stack([p, core, r]).astype(jnp.int32)

    rows = cycle_inter.shape[0]
    eighth = rows // 8
    sizes = [2 * eighth, 2 * eighth, 2 * eighth, eighth, eighth]
    starts = [sum(sizes[:i]) for i in range(len(sizes))]
    gathered = [
        lax.all_gather(cycle_inter[a : a + n], "col", axis=1, tiled=True)
        for a, n in zip(starts, sizes)
    ]

    t = jnp.transpose(doubles, (0, 1, 3, 2))
    to = 2 * (p ^ jnp.arange(planes, dtype=jnp.int32))
    give = pack((to + 1 - core).astype(jnp.int32), t, planes)
    got = lax.ppermute(give, "col", [(c, c ^ 1) for c in range(2 * planes)])
    packed = pack((to + core).astype(jnp.int32), t, planes, got)

    def across(x, bit):
        return lax.ppermute(x, "row", [(a, a ^ bit) for a in range(rows_r)])

    came = [[], [], [], []]
    for d in range(planes):
        x = packed[d]
        if d:
            pairs = [(2 * (q ^ d) + c, 2 * q + c) for q in range(planes) for c in range(2)]
            x = lax.ppermute(x, "col", pairs)
        one, two = across(x, 1), across(x, 2)
        came[0].append([x])
        came[1].append([one])
        came[2].append([two])
        came[3].append([across(one[:1], 2), across(two[1:], 1)])
    hilo = panel(where, came, planes, vb, k // planes, vr)

    result = None
    for a, start in zip(gathered, starts):
        result = product(a, hilo, result, start, rows)
    return result


def solution(mesh):
    rows_r, planes = mesh.shape["row"], mesh.shape["col"] // 2

    def body(doubles, cycle_inter):
        if rows_r == 2 * 2 and planes & (planes - 1) == 0:
            return line(doubles, cycle_inter, rows_r, planes)
        return plain(doubles, cycle_inter)

    placed = (P(None, None, "row", "col"), P("row", "col"))
    return jax.shard_map(
        body, mesh=mesh, in_specs=placed, out_specs=P("row", "col"), check_vma=False
    )
```

time: 911 us -> 498 us (0.55)
  blocking collectives: 205 us -> 0 us
  waiting for transfers between devices: 499 us -> 315 us
  Pallas kernels: 0 us -> 113 us
  matrix products: 101 us -> 0 us
  local copies, waits for them, and re-layouts: 74.8 us -> 25.2 us
  starting transfers between devices: 0.04 us -> 28.3 us
  other arithmetic: 16.9 us -> 0.09 us
    all_gather x2 -> x5, waiting for transfers between devices: 499 us -> 93.6 us  [line(): lax.all_gather(cycle_inter[a:a + n], 'col', axis=1, tiled=True)]
    ppermute x0 -> x20, waiting for transfers between devices: none -> 220 us  [the longest x3 134 us: line(): x = lax.ppermute(x, 'col', pairs)]
    all_to_all x2 -> x0, blocking collectives: 205 us -> none  [the longest x1 144 us: body(): lax.all_to_all(lax.all_to_all(doubles, 'row', split_axis=0, concat_axis=2...]
    pallas_call x0 -> x8, Pallas kernels: none -> 113 us  [the longest x5 80.1 us: product(): pl.pallas_call(kernel, grid=(depth // tk,), in_specs=specs, out_specs=pl....]
    dot_general x1 -> x0, matrix products: 101 us -> none  [body(): jnp.dot(lax.all_gather(cycle_inter, 'col', axis=1, tiled=True), amp_panel...]
    all_to_all x5 -> x0, local copies, waits for them, and re-layouts: 33.4 us -> none  [the longest x4 32.6 us: body(): lax.all_to_all(doubles, 'row', split_axis=0, concat_axis=2, tiled=True)]
    ppermute x0 -> x20, starting transfers between devices: none -> 28.1 us  [the longest x16 20.5 us: across(): return lax.ppermute(x, 'row', [(a, a ^ bit) for a in range(rows_r)])]
    all_to_all x1 -> x0, other arithmetic: 16.9 us -> none  [body(): lax.all_to_all(doubles, 'row', split_axis=0, concat_axis=2, tiled=True)]
  transfers between devices with their start and end apart: 2 -> 25, of which waited for: 2 -> 13; matrix products, arithmetic and copies ran while one was open for 0% -> 1% of each run, Pallas kernels for 0% -> 20%
where the time goes in v1:
time: 498 us; the launch traced here: 495 us
  waiting for transfers between devices  315 us (63%)
  Pallas kernels  113 us (23%)
  starting transfers between devices  28.3 us (6%)
  local copies, waits for them, and re-layouts  25.2 us (5%)
  between operations  13.3 us (3%)
    ppermute x3, waiting for transfers between devices, line(): x = lax.ppermute(x, 'col', pairs)  134 us
    all_gather x5, waiting for transfers between devices, line(): lax.all_gather(cycle_inter[a:a + n], 'col', axis=1, tiled=True)  93.6 us
    ppermute x16, waiting for transfers between devices, across(): return lax.ppermute(x, 'row', [(a, a ^ bit) for a in range(rows_r)])  81.6 us
    pallas_call x5, Pallas kernels, product(): pl.pallas_call(kernel, grid=(depth // tk,), in_specs=specs, out_specs=pl....  80.1 us
    pallas_call x1, Pallas kernels, panel(): pl.pallas_call(kernel, grid_spec=pltpu.PrefetchScalarGridSpec(num_scalar_...  22.4 us
    ppermute x16, starting transfers between devices, across(): return lax.ppermute(x, 'row', [(a, a ^ bit) for a in range(rows_r)])  20.5 us
    unnamed x40, local copies, waits for them, and re-layouts  14.5 us
    pallas_call x2, Pallas kernels, pack(): pl.pallas_call(kernel, grid_spec=pltpu.PrefetchScalarGridSpec(num_scalar_...  10.9 us
  transfers between devices with their start and end apart: 25, of which 13 were waited for; matrix products, arithmetic and copies ran while one was open for 1% of the time, Pallas kernels for 20%

profile of v1, /device:TPU:0, one launch (start us, length us, event | category | flops | bytes accessed | tf_op | source)
XLA Modules:
  0.0 495.4 jit_solution(731063597425148015)
XLA Ops:
  6.5 3.9 fusion.1
  14.4 6.0 %shard_map.28 = f32[4,96,1536]{2,1,0:T(8,128)} custom-call(s32[4]{0:T(128)S(1)} %add_subtract_fusion.blocks_ref, f32[32,32,24,48]{3,2,1,0:T(8,128)} %bitcast.4), custom_call_target="tpu_custom_call" | custom-call | bytes 5898240 | tf_op jit(solution)/shard_map/pallas_call | solution.py:64
  21.0 4.3 collective-permute-done.got_ref
  25.3 4.9 shard_map.29
  30.2 4.7 collective-permute-start.1
  34.9 2.5 collective-permute-start.2
  40.7 98.7 %collective-permute-done.1.refs_1_ = f32[2,96,1536]{2,1,0:T(8,128)S(1)} collective-permute-done((f32[2,96,1536]{2,1,0:T(8,128)S(1)}, f32[2,96,1536]{2,1,0:T(8,128)S(1)}, u32[]{:S(2)}, u32[]{:S(2)}) %collective-permute-start.1) | collective-permute-done | bytes 1179680 | tf_op jit(solution)/shard_map/ppermute | solution.py:227
  140.9 6.8 %collective-permute-done.2.refs_2_ = f32[2,96,1536]{2,1,0:T(8,128)S(1)} collective-permute-done((f32[2,96,1536]{2,1,0:T(8,128)S(1)}, f32[2,96,1536]{2,1,0:T(8,128)S(1)}, u32[]{:S(2)}, u32[]{:S(2)}) %collective-permute-start.2) | collective-permute-done | bytes 1179680 | tf_op jit(solution)/shard_map/ppermute | solution.py:227
  149.3 28.8 %collective-permute-done.3.refs_3_ = f32[2,96,1536]{2,1,0:T(8,128)S(1)} collective-permute-done((f32[2,96,1536]{2,1,0:T(8,128)S(1)}, f32[2,96,1536]{2,1,0:T(8,128)S(1)}, u32[]{:S(2)}, u32[]{:S(2)}) %collective-permute-start.3) | collective-permute-done | bytes 1179680 | tf_op jit(solution)/shard_map/ppermute | solution.py:227
  185.9 21.0 %collective-permute-done.6.refs_6_ = f32[2,96,1536]{2,1,0:T(8,128)S(1)} collective-permute-done((f32[2,96,1536]{2,1,0:T(8,128)S(1)}, f32[2,96,1536]{2,1,0:T(8,128)S(1)}, u32[]{:S(2)}, u32[]{:S(2)}) %collective-permute-start.6) | collective-permute-done | bytes 1179680 | tf_op jit(solution)/shard_map/ppermute | solution.py:220
  212.5 19.6 %collective-permute-done.7.refs_7_ = f32[2,96,1536]{2,1,0:T(8,128)S(1)} collective-permute-done((f32[2,96,1536]{2,1,0:T(8,128)S(1)}, f32[2,96,1536]{2,1,0:T(8,128)S(1)}, u32[]{:S(2)}, u32[]{:S(2)}) %collective-permute-start.7) | collective-permute-done | bytes 1179680 | tf_op jit(solution)/shard_map/ppermute | solution.py:220
  236.9 9.5 %collective-permute-done.12.refs_12_ = f32[1,96,1536]{2,1,0:T(8,128)S(1)} collective-permute-done((f32[1,96,1536]{2,1,0:T(8,128)S(1)}, f32[1,96,1536]{2,1,0:T(8,128)S(1)}, u32[]{:S(2)}, u32[]{:S(2)}) %collective-permute-start.12) | collective-permute-done | bytes 589856 | tf_op jit(solution)/shard_map/ppermute | solution.py:220
  250.0 9.0 %collective-permute-done.14.refs_14_ = f32[1,96,1536]{2,1,0:T(8,128)S(1)} collective-permute-done((f32[1,96,1536]{2,1,0:T(8,128)S(1)}, f32[1,96,1536]{2,1,0:T(8,128)S(1)}, u32[]{:S(2)}, u32[]{:S(2)}) %collective-permute-start.14) | collective-permute-done | bytes 589856 | tf_op jit(solution)/shard_map/ppermute | solution.py:220
  260.5 11.3 %collective-permute-done.16.refs_16_ = f32[1,96,1536]{2,1,0:T(8,128)} collective-permute-done((f32[1,96,1536]{2,1,0:T(8,128)}, f32[1,96,1536]{2,1,0:T(8,128)}, u32[]{:S(2)}, u32[]{:S(2)}) %collective-permute-start.16) | collective-permute-done | bytes 589856 | tf_op jit(solution)/shard_map/ppermute | solution.py:220
  271.7 11.2 %collective-permute-done.18.refs_18_ = f32[1,96,1536]{2,1,0:T(8,128)} collective-permute-done((f32[1,96,1536]{2,1,0:T(8,128)}, f32[1,96,1536]{2,1,0:T(8,128)}, u32[]{:S(2)}, u32[]{:S(2)}) %collective-permute-start.18) | collective-permute-done | bytes 589856 | tf_op jit(solution)/shard_map/ppermute | solution.py:220
  292.8 22.4 %shard_map.30 = (bf16[768,6144]{1,0:T(8,128)(2,1)}, bf16[768,6144]{1,0:T(8,128)(2,1)}) custom-call(s32[3]{0:T(128)S(1)} %pad_add_fusion.w_ref, f32[2,96,1536]{2,1,0:T(8,128)S(1)} %copy-done.3, f32[2,96,1536]{2,1,0:T(8,128)S(1)} %copy-done.5, f32[2,96,1536]{2,1,0:T(8,128)S(1)} %copy-done.7, f32[2,96,1536]{2,1,0:T(8,128)S(1)} %copy-done.9, ...), custom_call_target="tpu_custom_call" | custom-call | bytes 37748736 | tf_op jit(solution)/shard_map/pallas_call | solution.py:118
  315.2 17.4 %shard_map.31.refs_0_ = f32[1536,768]{1,0:T(8,128)} custom-call(f32[384,6144]{1,0:T(8,128)} %all-gather.14.cloned.1.call-done.a_ref, bf16[768,6144]{1,0:T(8,128)(2,1)} %get-tuple-element.15.h_ref, bf16[768,6144]{1,0:T(8,128)(2,1)} %get-tuple-element.16.l_ref), custom_call_target="tpu_custom_call" | custom-call | flops 10871635968 | bytes 28311552 | tf_op jit(solution)/shard_map/pallas_call | solution.py:166
  332.7 17.4 %shard_map.32.refs_0_ = f32[1536,768]{1,0:T(8,128)} custom-call(f32[384,6144]{1,0:T(8,128)} %all-gather.12.cloned.1.call-done.a_ref, bf16[768,6144]{1,0:T(8,128)(2,1)} %get-tuple-element.15.h_ref, bf16[768,6144]{1,0:T(8,128)(2,1)} %get-tuple-element.16.l_ref, f32[1536,768]{1,0:T(8,128)} %shard_map.31.refs_0_), custom_call_target="tpu_custom_call", output_to_operand_aliasing={{}: (3, {})} | custom-call | flops 10871635968 | bytes 28311552 | tf_op jit(solution)/shard_map/pallas_call | solution.py:166
  350.1 21.5 %all-gather.10.cloned.1.call-done.a_ref = f32[384,6144]{1,0:T(8,128)} async-done(((f32[384,768]{1,0:T(8,128)}), f32[384,6144]{1,0:T(8,128)}) %all-gather.10.cloned.1.call-update) | async-done | bytes 9437200 | tf_op jit(solution)/shard_map/all_gather | solution.py:209
  371.6 17.6 %shard_map.33.refs_0_ = f32[1536,768]{1,0:T(8,128)} custom-call(f32[384,6144]{1,0:T(8,128)} %all-gather.10.cloned.1.call-done.a_ref, bf16[768,6144]{1,0:T(8,128)(2,1)} %get-tuple-element.15.h_ref, bf16[768,6144]{1,0:T(8,128)(2,1)} %get-tuple-element.16.l_ref, f32[1536,768]{1,0:T(8,128)} %shard_map.32.refs_0_), custom_call_target="tpu_custom_call", output_to_operand_aliasing={{}: (3, {})} | custom-call | flops 10871635968 | bytes 28311552 | tf_op jit(solution)/shard_map/pallas_call | solution.py:166
  389.3 33.9 %all-gather.8.cloned.1.call-done.a_ref = f32[192,6144]{1,0:T(8,128)} async-done(((f32[192,768]{1,0:T(8,128)}), f32[192,6144]{1,0:T(8,128)}) %all-gather.8.cloned.1.call-update) | async-done | bytes 4718608 | tf_op jit(solution)/shard_map/all_gather | solution.py:209
  423.2 13.9 %shard_map.34.refs_0_ = f32[1536,768]{1,0:T(8,128)} custom-call(f32[192,6144]{1,0:T(8,128)} %all-gather.8.cloned.1.call-done.a_ref, bf16[768,6144]{1,0:T(8,128)(2,1)} %get-tuple-element.15.h_ref, bf16[768,6144]{1,0:T(8,128)(2,1)} %get-tuple-element.16.l_ref, f32[1536,768]{1,0:T(8,128)} %shard_map.33.refs_0_), custom_call_target="tpu_custom_call", output_to_operand_aliasing={{}: (3, {})} | custom-call | flops 5435817984 | bytes 23592960 | tf_op jit(solution)/shard_map/pallas_call | solution.py:166
  437.1 38.1 %all-gather.6.cloned.1.call-done.a_ref = f32[192,6144]{1,0:T(8,128)} async-done(((f32[192,768]{1,0:T(8,128)}), f32[192,6144]{1,0:T(8,128)}) %all-gather.6.cloned.1.call-update) | async-done | bytes 4718608 | tf_op jit(solution)/shard_map/all_gather | solution.py:209
  475.2 13.7 %shard_map.35 = f32[1536,768]{1,0:T(8,128)} custom-call(f32[192,6144]{1,0:T(8,128)} %all-gather.6.cloned.1.call-done.a_ref, bf16[768,6144]{1,0:T(8,128)(2,1)} %get-tuple-element.15.h_ref, bf16[768,6144]{1,0:T(8,128)(2,1)} %get-tuple-element.16.l_ref, f32[1536,768]{1,0:T(8,128)} %shard_map.34.refs_0_), custom_call_target="tpu_custom_call", output_to_operand_aliasing={{}: (3, {})} | custom-call | flops 5435817984 | bytes 23592960 | tf_op jit(solution)/shard_map/pallas_call | solution.py:166
  (92 shorter events, 44.0 us)
Async XLA Ops:
  6.5 308.7 %all-gather.14.cloned.1.call-start = ((), (), s32[]{:S(2)}) async-start(), calls=%async_computation.4 | async-start | bytes 10616832 | tf_op jit(solution)/shard_map/all_gather | solution.py:209
  10.5 322.2 %all-gather.12.cloned.1.call-start = ((), (), s32[]{:S(2)}) async-start(), calls=%async_computation.3 | async-start | bytes 10616832 | tf_op jit(solution)/shard_map/all_gather | solution.py:209
  11.2 360.4 %all-gather.10.cloned.1.call-start = ((), (), s32[]{:S(2)}) async-start(), calls=%async_computation.2 | async-start | bytes 10616832 | tf_op jit(solution)/shard_map/all_gather | solution.py:209
  11.9 411.3 %all-gather.8.cloned.1.call-start = ((), (), s32[]{:S(2)}) async-start(), calls=%async_computation.1 | async-start | bytes 5308416 | tf_op jit(solution)/shard_map/all_gather | solution.py:209
  14.4 460.9 %all-gather.6.cloned.1.call-start = ((), (), s32[]{:S(2)}) async-start(), calls=%async_computation | async-start | bytes 5308416 | tf_op jit(solution)/shard_map/all_gather | solution.py:209
  30.2 109.2 %collective-permute-start.1 = (f32[2,96,1536]{2,1,0:T(8,128)S(1)}, f32[2,96,1536]{2,1,0:T(8,128)S(1)}, u32[]{:S(2)}, u32[]{:S(2)}) collective-permute-start(f32[2,96,1536]{2,1,0:T(8,128)S(1)} %get-tuple-element.12), channel_id=1, source_target_pairs={{2,0},{3,1},{0,2},{1,3},{6,4},{7,5},{4,6},{5,7},{10,8},{11,9},{8,1... | collective-permute-start | bytes 3538952 | tf_op jit(solution)/shard_map/ppermute | solution.py:227
  34.9 112.8 %collective-permute-start.2 = (f32[2,96,1536]{2,1,0:T(8,128)S(1)}, f32[2,96,1536]{2,1,0:T(8,128)S(1)}, u32[]{:S(2)}, u32[]{:S(2)}) collective-permute-start(f32[2,96,1536]{2,1,0:T(8,128)S(1)} %get-tuple-element.13), channel_id=1, source_target_pairs={{4,0},{5,1},{6,2},{7,3},{0,4},{1,5},{2,6},{3,7},{12,8},{13,9},{14,... | collective-permute-start | bytes 3538952 | tf_op jit(solution)/shard_map/ppermute | solution.py:227
  37.4 140.6 %collective-permute-start.3 = (f32[2,96,1536]{2,1,0:T(8,128)S(1)}, f32[2,96,1536]{2,1,0:T(8,128)S(1)}, u32[]{:S(2)}, u32[]{:S(2)}) collective-permute-start(f32[2,96,1536]{2,1,0:T(8,128)S(1)} %get-tuple-element.14), channel_id=1, source_target_pairs={{6,0},{7,1},{4,2},{5,3},{2,4},{3,5},{0,6},{1,7},{14,8},{15,9},{12,... | collective-permute-start | bytes 3538952 | tf_op jit(solution)/shard_map/ppermute | solution.py:227
  37.4 142.1 %collective-permute-start.4 = (f32[2,96,1536]{2,1,0:T(8,128)S(1)}, f32[2,96,1536]{2,1,0:T(8,128)S(1)}, u32[]{:S(2)}, u32[]{:S(2)}) collective-permute-start(f32[2,96,1536]{2,1,0:T(8,128)S(1)} %get-tuple-element.11.refs_0_), channel_id=1, source_target_pairs={{0,8},{8,0},{16,24},{24,16},{1,9},{9,1},{17,25},{25,17},{2,10},{10... | collective-permute-start | bytes 3538952 | tf_op jit(solution)/shard_map/ppermute | solution.py:220
  39.2 142.8 %collective-permute-start.8 = (f32[2,96,1536]{2,1,0:T(8,128)S(1)}, f32[2,96,1536]{2,1,0:T(8,128)S(1)}, u32[]{:S(2)}, u32[]{:S(2)}) collective-permute-start(f32[2,96,1536]{2,1,0:T(8,128)S(1)} %get-tuple-element.11.refs_0_), channel_id=1, source_target_pairs={{0,16},{8,24},{16,0},{24,8},{1,17},{9,25},{17,1},{25,9},{2,18},{10... | collective-permute-start | bytes 3538952 | tf_op jit(solution)/shard_map/ppermute | solution.py:220
  139.4 43.2 %collective-permute-start.5 = (f32[2,96,1536]{2,1,0:T(8,128)S(1)}, f32[2,96,1536]{2,1,0:T(8,128)S(1)}, u32[]{:S(2)}, u32[]{:S(2)}) collective-permute-start(f32[2,96,1536]{2,1,0:T(8,128)S(1)} %collective-permute-done.1.refs_1_), channel_id=1, source_target_pairs={{0,8},{8,0},{16,24},{24,16},{1,9},{9,1},{17,25},{25,17},{2,10},{10... | collective-permute-start | bytes 3538952 | tf_op jit(solution)/shard_map/ppermute | solution.py:220
  147.7 36.6 %collective-permute-start.9 = (f32[2,96,1536]{2,1,0:T(8,128)S(1)}, f32[2,96,1536]{2,1,0:T(8,128)S(1)}, u32[]{:S(2)}, u32[]{:S(2)}) collective-permute-start(f32[2,96,1536]{2,1,0:T(8,128)S(1)} %collective-permute-done.1.refs_1_), channel_id=1, source_target_pairs={{0,16},{8,24},{16,0},{24,8},{1,17},{9,25},{17,1},{25,9},{2,18},{10... | collective-permute-start | bytes 3538952 | tf_op jit(solution)/shard_map/ppermute | solution.py:220
  178.1 28.9 %collective-permute-start.6 = (f32[2,96,1536]{2,1,0:T(8,128)S(1)}, f32[2,96,1536]{2,1,0:T(8,128)S(1)}, u32[]{:S(2)}, u32[]{:S(2)}) collective-permute-start(f32[2,96,1536]{2,1,0:T(8,128)S(1)} %collective-permute-done.2.refs_2_), channel_id=1, source_target_pairs={{0,8},{8,0},{16,24},{24,16},{1,9},{9,1},{17,25},{25,17},{2,10},{10... | collective-permute-start | bytes 3538952 | tf_op jit(solution)/shard_map/ppermute | solution.py:220
  179.5 28.9 %collective-permute-start.10 = (f32[2,96,1536]{2,1,0:T(8,128)S(1)}, f32[2,96,1536]{2,1,0:T(8,128)S(1)}, u32[]{:S(2)}, u32[]{:S(2)}) collective-permute-start(f32[2,96,1536]{2,1,0:T(8,128)S(1)} %collective-permute-done.2.refs_2_), channel_id=1, source_target_pairs={{0,16},{8,24},{16,0},{24,8},{1,17},{9,25},{17,1},{25,9},{2,18},{10... | collective-permute-start | bytes 3538952 | tf_op jit(solution)/shard_map/ppermute | solution.py:220
  182.0 50.2 %collective-permute-start.7 = (f32[2,96,1536]{2,1,0:T(8,128)S(1)}, f32[2,96,1536]{2,1,0:T(8,128)S(1)}, u32[]{:S(2)}, u32[]{:S(2)}) collective-permute-start(f32[2,96,1536]{2,1,0:T(8,128)S(1)} %collective-permute-done.3.refs_3_), channel_id=1, source_target_pairs={{0,8},{8,0},{16,24},{24,16},{1,9},{9,1},{17,25},{25,17},{2,10},{10... | collective-permute-start | bytes 3538952 | tf_op jit(solution)/shard_map/ppermute | solution.py:220
  182.6 51.9 %collective-permute-start.11 = (f32[2,96,1536]{2,1,0:T(8,128)S(1)}, f32[2,96,1536]{2,1,0:T(8,128)S(1)}, u32[]{:S(2)}, u32[]{:S(2)}) collective-permute-start(f32[2,96,1536]{2,1,0:T(8,128)S(1)} %collective-permute-done.3.refs_3_), channel_id=1, source_target_pairs={{0,16},{8,24},{16,0},{24,8},{1,17},{9,25},{17,1},{25,9},{2,18},{10... | collective-permute-start | bytes 3538952 | tf_op jit(solution)/shard_map/ppermute | solution.py:220
  184.4 62.0 %collective-permute-start.12 = (f32[1,96,1536]{2,1,0:T(8,128)S(1)}, f32[1,96,1536]{2,1,0:T(8,128)S(1)}, u32[]{:S(2)}, u32[]{:S(2)}) collective-permute-start(f32[1,96,1536]{2,1,0:T(8,128)S(1)} %slice.52), channel_id=1, source_target_pairs={{0,16},{8,24},{16,0},{24,8},{1,17},{9,25},{17,1},{25,9},{2,18},{10... | collective-permute-start | bytes 1769480 | tf_op jit(solution)/shard_map/ppermute | solution.py:220
  206.9 40.8 %collective-permute-start.13 = (f32[1,96,1536]{2,1,0:T(8,128)S(1)}, f32[1,96,1536]{2,1,0:T(8,128)S(1)}, u32[]{:S(2)}, u32[]{:S(2)}) collective-permute-start(f32[1,96,1536]{2,1,0:T(8,128)S(1)} %slice.53), channel_id=1, source_target_pairs={{0,8},{8,0},{16,24},{24,16},{1,9},{9,1},{17,25},{25,17},{2,10},{10... | collective-permute-start | bytes 1769480 | tf_op jit(solution)/shard_map/ppermute | solution.py:220
  208.4 50.6 %collective-permute-start.14 = (f32[1,96,1536]{2,1,0:T(8,128)S(1)}, f32[1,96,1536]{2,1,0:T(8,128)S(1)}, u32[]{:S(2)}, u32[]{:S(2)}) collective-permute-start(f32[1,96,1536]{2,1,0:T(8,128)S(1)} %slice.54), channel_id=1, source_target_pairs={{0,16},{8,24},{16,0},{24,8},{1,17},{9,25},{17,1},{25,9},{2,18},{10... | collective-permute-start | bytes 1769480 | tf_op jit(solution)/shard_map/ppermute | solution.py:220
  232.2 28.3 %collective-permute-start.15 = (f32[1,96,1536]{2,1,0:T(8,128)}, f32[1,96,1536]{2,1,0:T(8,128)}, u32[]{:S(2)}, u32[]{:S(2)}) collective-permute-start(f32[1,96,1536]{2,1,0:T(8,128)} %slice.55), channel_id=1, source_target_pairs={{0,8},{8,0},{16,24},{24,16},{1,9},{9,1},{17,25},{25,17},{2,10},{10... | collective-permute-start | bytes 1769480 | tf_op jit(solution)/shard_map/ppermute | solution.py:220
  234.5 37.2 %collective-permute-start.16 = (f32[1,96,1536]{2,1,0:T(8,128)}, f32[1,96,1536]{2,1,0:T(8,128)}, u32[]{:S(2)}, u32[]{:S(2)}) collective-permute-start(f32[1,96,1536]{2,1,0:T(8,128)} %slice.56), channel_id=1, source_target_pairs={{0,16},{8,24},{16,0},{24,8},{1,17},{9,25},{17,1},{25,9},{2,18},{10... | collective-permute-start | bytes 1769480 | tf_op jit(solution)/shard_map/ppermute | solution.py:220
  247.2 24.6 %collective-permute-start.17 = (f32[1,96,1536]{2,1,0:T(8,128)}, f32[1,96,1536]{2,1,0:T(8,128)}, u32[]{:S(2)}, u32[]{:S(2)}) collective-permute-start(f32[1,96,1536]{2,1,0:T(8,128)} %slice.57), channel_id=1, source_target_pairs={{0,8},{8,0},{16,24},{24,16},{1,9},{9,1},{17,25},{25,17},{2,10},{10... | collective-permute-start | bytes 1769480 | tf_op jit(solution)/shard_map/ppermute | solution.py:220
  248.5 34.4 %collective-permute-start.18 = (f32[1,96,1536]{2,1,0:T(8,128)}, f32[1,96,1536]{2,1,0:T(8,128)}, u32[]{:S(2)}, u32[]{:S(2)}) collective-permute-start(f32[1,96,1536]{2,1,0:T(8,128)} %slice.58), channel_id=1, source_target_pairs={{0,16},{8,24},{16,0},{24,8},{1,17},{9,25},{17,1},{25,9},{2,18},{10... | collective-permute-start | bytes 1769480 | tf_op jit(solution)/shard_map/ppermute | solution.py:220
  259.8 23.1 %collective-permute-start.19 = (f32[1,96,1536]{2,1,0:T(8,128)}, f32[1,96,1536]{2,1,0:T(8,128)}, u32[]{:S(2)}, u32[]{:S(2)}) collective-permute-start(f32[1,96,1536]{2,1,0:T(8,128)} %slice.59), channel_id=1, source_target_pairs={{0,8},{8,0},{16,24},{24,16},{1,9},{9,1},{17,25},{25,17},{2,10},{10... | collective-permute-start | bytes 1769480 | tf_op jit(solution)/shard_map/ppermute | solution.py:220
  (21 other events, 308.4 us)
Sparse Core Ops, SparseCore 0:
  10.6 175.4 all-gather.13
  187.7 93.0 all-gather.11
  282.5 89.0 all-gather.9
  373.1 50.0 all-gather.7
  424.7 50.5 all-gather.5

commit v2 on v0

v2 whole, which is shorter than its diff:
```python
import functools

import jax
import jax.numpy as jnp
from jax import lax
from jax.experimental import pallas as pl
from jax.experimental.pallas import tpu as pltpu
from jax.sharding import PartitionSpec as P


NT = (((1,), (1,)), ((), ()))
SIZES = (2, 2, 2, 2)


def params(mib):
    return pltpu.CompilerParams(vmem_limit_bytes=mib * 2**20)


def cost(flops, moved):
    return pl.CostEstimate(flops=flops // 4096, bytes_accessed=moved // 4096, transcendentals=0)


def after(x, *deps):
    return lax.optimization_barrier((x,) + deps)[0]


def pack(steps, t, planes, classes, received=None):
    k, j, vb, vr = t.shape
    kp = k // planes
    jl = j // (2 * planes)
    rows, lanes = jl * vb, k // 2 * vr
    kl = kp // 2
    ks = [
        [q * kp + of * kl + i for of in range(2) for q in c for i in range(kl)]
        for c in classes
    ]

    def fill(s_ref, t_ref, put):
        step = pl.program_id(0)
        for c in range(2):

            @pl.when(s_ref[2 * planes + step] == c)
            def _():
                for jj in range(jl):
                    put(
                        jj * vb,
                        jnp.concatenate([t_ref[kk, jj] for kk in ks[c]], axis=-1),
                    )

    def give(s_ref, t_ref, o_ref):
        def put(at, x):
            o_ref[0, at : at + vb] = x

        fill(s_ref, t_ref, put)

    def merge(s_ref, t_ref, got_ref, *outs):
        step = pl.program_id(0)
        first = pl.multiple_of(step % 2 * rows, rows)
        for d in range(planes):

            @pl.when(step // 2 == d)
            def _():
                def put(at, x):
                    outs[d][0, pl.ds(first + at, vb)] = x

                fill(s_ref, t_ref, put)
                outs[d][1, pl.ds(first, rows)] = got_ref[0]

    t_spec = pl.BlockSpec((k, jl, vb, vr), lambda i, b: (0, b[i], 0, 0))
    given = pl.BlockSpec((1, rows, lanes), lambda i, b: (i // 2, i % 2, 0))
    if received is None:
        kernel, args, ins, outs = give, (), [t_spec], given
        shape = jax.ShapeDtypeStruct((planes, 2 * rows, lanes), t.dtype)
    else:
        kernel, args, ins = merge, (received,), [t_spec, given]
        outs = [pl.BlockSpec((2, 2 * rows, lanes), lambda i, b: (0, 0, 0))] * planes
        shape = [jax.ShapeDtypeStruct((2, 2 * rows, lanes), t.dtype)] * planes
    return pl.pallas_call(
        kernel,
        grid_spec=pltpu.PrefetchScalarGridSpec(
            num_scalar_prefetch=1, grid=(2 * planes,), in_specs=ins, out_specs=outs
        ),
        out_shape=shape,
        compiler_params=params(40),
        cost_estimate=cost(0, 5 * t.size),
    )(steps, t, *args)


def panel(where, d, came, into, planes, vb, kp, vr):
    rows_r = len(came)
    rows, lanes = came[0][0][0].shape[1:]
    nj = rows // vb
    lw = kp * vr
    pieces = [x for e in came for x in e]
    arrays = [x for x, _, _ in pieces]
    index = []
    for n, (e, count) in enumerate((e, x[2]) for e in range(rows_r) for x in came[e]):
        index += [(e, n, i) for i in range(count)]

    def kernel(w_ref, *refs):
        hi_ref, lo_ref, x_ref = refs[-3:]
        core, r = w_ref[1], w_ref[2]
        for i, (e, n, first) in enumerate(index):
            to = pl.multiple_of((core ^ (i % 2)) * vb, vb)
            x_ref[r ^ e, pl.ds(to, vb)] = refs[n][first]
        for k in range(0, kp, 2):
            x = jnp.concatenate(
                [
                    x_ref[q, :, (k + kk) * vr : (k + kk + 1) * vr]
                    for kk in range(2)
                    for q in range(rows_r)
                ],
                axis=-1,
            )
            at = slice(k * rows_r * vr, (k + 2) * rows_r * vr)
            hi = x.astype(jnp.bfloat16)
            hi_ref[:, at] = hi
            lo_ref[:, at] = (x - hi.astype(jnp.float32)).astype(jnp.bfloat16)

    out = pl.BlockSpec((2 * vb, rows_r * lw), lambda t, j, w: (j * planes + (w[0] ^ d), t))
    shape = jax.ShapeDtypeStruct((nj * planes * 2 * vb, rows_r * lanes), jnp.bfloat16)

    def spec(at, count):
        return pl.BlockSpec((count, vb, lw), lambda t, j, w: (at // count, j, t))

    specs = [spec(at, count) for _, at, count in pieces]
    alias = {}
    if into is not None:
        alias = {1 + len(arrays): 0, 2 + len(arrays): 1}
        specs += [pl.BlockSpec(memory_space=pl.ANY)] * 2
        arrays = arrays + list(into)
    return pl.pallas_call(
        kernel,
        grid_spec=pltpu.PrefetchScalarGridSpec(
            num_scalar_prefetch=1,
            grid=(lanes // lw, nj),
            in_specs=specs,
            out_specs=[out, out],
            scratch_shapes=[pltpu.VMEM((rows_r, 2 * vb, lw), jnp.float32)],
        ),
        out_shape=[shape, shape],
        input_output_aliases=alias,
        compiler_params=params(40),
        cost_estimate=cost(0, 16 * nj * vb * rows_r * lanes),
    )(where, *arrays)


def product(where, m, offsets, own, other, hilo):
    hi, lo = hilo
    n, depth = hi.shape
    n //= 2
    per = len(offsets)
    tk = depth // (2 * per)
    operands = own + other

    def kernel(w_ref, *refs):
        ins, (h_ref, l_ref), outs = refs[: 2 * per], refs[2 * per : 2 * per + 2], refs[-3:-1]
        x_ref = refs[-1]
        step = pl.program_id(0)

        @pl.when(step == 0)
        def _():
            for o in outs:
                o[...] = jnp.zeros_like(o)

        for i, ref in enumerate(ins):

            @pl.when(step == i)
            def _():
                x = ref[...]
                xh = x.astype(jnp.bfloat16)
                x_ref[:m] = xh
                x_ref[m:] = (x - xh.astype(jnp.float32)).astype(jnp.bfloat16)

        dot = functools.partial(
            lax.dot_general, dimension_numbers=NT, preferred_element_type=jnp.float32
        )
        for i, o in enumerate(outs):
            at = slice(i * n, (i + 1) * n)
            both = dot(x_ref[...], h_ref[at])
            o[...] += both[:m] + both[m:] + dot(x_ref[:m], l_ref[at])

    def block(i, w):
        plane = w[0] ^ offsets[0]
        for n in range(1, per):
            plane = jnp.where(i % per == n, w[0] ^ offsets[n], plane)
        return 0, per * (w[1] ^ (i // per)) + plane // 2

    def rows(chunk):
        return pl.BlockSpec((m, tk), lambda i, w: (chunk, 0))

    out = pl.BlockSpec((m, n), lambda i, w: (0, 0))
    return pl.pallas_call(
        kernel,
        grid_spec=pltpu.PrefetchScalarGridSpec(
            num_scalar_prefetch=1,
            grid=(2 * per,),
            in_specs=[rows(c) for _, c in operands]
            + [pl.BlockSpec((2 * n, tk), block)] * 2,
            out_specs=[out, out],
            scratch_shapes=[pltpu.VMEM((2 * m, tk), jnp.bfloat16)],
        ),
        out_shape=[jax.ShapeDtypeStruct((m, n), jnp.float32)] * 2,
        compiler_params=params(52),
        cost_estimate=cost(12 * m * n * depth, 4 * m * depth + 8 * n * depth),
    )(where, *[x for x, _ in operands], hi, lo)


def finish(x, y, into, start, m, rows):
    n = x.shape[1]
    tm = m // 2

    def kernel(x_ref, y_ref, *refs):
        refs[-1][...] = x_ref[...] + y_ref[...]

    specs = [pl.BlockSpec((tm, n), lambda i: (i, 0))] * 2
    args, alias = [x, y], {}
    if into is not None:
        args.append(into)
        specs.append(pl.BlockSpec(memory_space=pl.ANY))
        alias = {2: 0}
    return pl.pallas_call(
        kernel,
        grid=(2,),
        in_specs=specs,
        out_specs=pl.BlockSpec((tm, n), lambda i: (start // tm + i, 0)),
        out_shape=jax.ShapeDtypeStruct((rows, n), jnp.float32),
        input_output_aliases=alias,
        compiler_params=params(40),
        cost_estimate=cost(m * n, 12 * m * n),
    )(*args)


def plain(doubles, cycle_inter):
    vs = doubles.shape[2] * lax.axis_size("row")
    moved = lax.all_to_all(
        lax.all_to_all(doubles, "row", split_axis=0, concat_axis=2, tiled=True),
        "col",
        split_axis=1,
        concat_axis=3,
        tiled=True,
    )
    local_panel = jnp.transpose(moved, (0, 2, 1, 3)).reshape(moved.shape[0] * vs, -1)
    amp_panel = lax.all_gather(local_panel, "row", axis=0, tiled=True)
    return jnp.dot(
        lax.all_gather(cycle_inter, "col", axis=1, tiled=True),
        amp_panel,
        precision=lax.Precision.HIGHEST,
        preferred_element_type=jnp.float32,
    )


def line(doubles, cycle_inter, rows_r, planes):
    k, j, vr, vb = doubles.shape
    col, r = lax.axis_index("col"), lax.axis_index("row")
    p, core = col // 2, col % 2
    where = jnp.stack([p, core, r]).astype(jnp.int32)
    kind = [(q ^ (2 * q // planes)) & 1 for q in range(planes)]
    classes = [[q for q in range(planes) if kind[q] == c] for c in range(2)]

    def send(x, pairs):
        pairs = [(2 * a + c, 2 * b + c) for a, b in pairs for c in range(2)]
        return lax.ppermute(x, "col", pairs)

    def swap(x):
        return lax.ppermute(x, "col", [(c, c ^ 1) for c in range(2 * planes)])

    trail = []

    def cross(x, d):
        x = after(x, *trail[-1:])
        trail.append(send(x, [(q ^ d, q) for q in range(planes)]))
        return trail[-1]

    rows = cycle_inter.shape[0]
    eighth = rows // 8
    sizes = [n * eighth for n in SIZES]
    starts = [sum(sizes[:i]) for i in range(len(sizes))]
    offsets = [d for d in range(planes) if kind[d] == 0]

    def take(start, size, *held):
        x = cycle_inter[start : start + size]
        return [cross(after(x, *held), d) for d in offsets[1:]]

    early = [take(0, eighth), take(eighth, sizes[0] - eighth)]
    gathered = [[jnp.concatenate(x) for x in zip(*early)]]

    t = jnp.transpose(doubles, (0, 1, 3, 2))
    to = (p ^ jnp.arange(planes, dtype=jnp.int32))[:, None] ^ jnp.arange(2)
    to_kind = jnp.take(jnp.array(kind), jnp.repeat(to[:, 0], 2))

    def steps(c):
        return jnp.concatenate([2 * to.reshape(-1) + c, to_kind]).astype(jnp.int32)

    give = pack(steps(1 - core), t, planes, classes)
    got = swap(give)
    packed = pack(steps(core), t, planes, classes, got)

    def across(x, bit):
        return lax.ppermute(x, "row", [(a, a ^ bit) for a in range(rows_r)])

    order = [0, 1] + list(range(planes - 1, 1, -1))
    parts = [packed[0]] + [None] * (planes - 1)
    links = [1 << i for i in range(rows_r.bit_length() - 1)]
    brought, hilos, hilo = [], [], None

    def block(n, e):
        if e == 0:
            return [(parts[n], 0, 2)]
        if e in links:
            return [(brought[n][e], 0, 2)]
        return [(brought[n + 1][link], 2 if n + 1 < planes else 0, 1) for link in links[::-1]]

    for n in range(planes + 1):
        if n < planes:
            d = order[n]
            if n == 1:
                x = after(packed[d], *early[0])
                parts[n] = send(x, [(q ^ d, q) for q in range(planes)])
            elif n:
                parts[n] = cross(packed[d], d)
            x = parts[n]
        else:
            gathered += [take(starts[1], sizes[1])]
        held = hilos[n - 3] if n > 2 else ()
        now = {}
        for i, link in enumerate(links):
            y = [x] if n < planes else []
            if n:
                y.append(brought[n - 1][links[1 - i]][1 - i : 2 - i])
            y = jnp.concatenate(y) if len(y) > 1 else y[0]
            now[link] = across(after(y, *held), link)
        brought.append(now)
        if n:
            pieces = [block(n - 1, e) for e in range(rows_r)]
            hilo = panel(
                where, order[n - 1], pieces, hilo, planes, vb, k // planes, vr
            )
            hilos.append(hilo)
    last = brought[-1].values()
    gathered += [take(starts[i], sizes[i], *last) for i in range(2, len(sizes))]

    result = None
    done, back = hilos[0][0], []
    own_other = swap(cycle_inter)
    for i, came in enumerate(gathered):
        came = [after(x, done) for x in came]
        other = [swap(x) for x in came]
        pieces = 1 if i + 1 < len(sizes) else 2
        m = sizes[i] // pieces
        for piece in range(pieces):
            start = starts[i] + piece * m
            came = [after(x, *back[: -1 - piece], done) for x in came]
            mine, theirs = product(
                where,
                m,
                offsets,
                [(cycle_inter, start // m)] + [(x, piece) for x in came],
                [(own_other, start // m)] + [(x, piece) for x in other],
                hilo,
            )
            done = mine
            back.append(send(theirs, [(q ^ 1, q) for q in range(planes)]))
            result = finish(mine, back[-1], result, start, m, rows)
    return result


def solution(mesh):
    rows_r, planes = mesh.shape["row"], mesh.shape["col"] // 2

    def body(doubles, cycle_inter):
        k, j, vr, vb = doubles.shape
        whole = vb % 8 == 0 and (2 * rows_r * vr) % 128 == 0 and (k // 2 * vr) % 128 == 0
        whole = whole and j % (2 * planes) == 0 and k // planes % 2 == 0
        if whole and planes > 1 and planes & (planes - 1) == 0 and rows_r == 2 * 2:
            return line(doubles, cycle_inter, rows_r, planes)
        return plain(doubles, cycle_inter)

    placed = (P(None, None, "row", "col"), P("row", "col"))
    return jax.shard_map(
        body, mesh=mesh, in_specs=placed, out_specs=P("row", "col"), check_vma=False
    )
```

time: 911 us -> 438 us (0.48)
  waiting for transfers between devices: 499 us -> 154 us
  blocking collectives: 205 us -> 0 us
  Pallas kernels: 0 us -> 142 us
  starting transfers between devices: 0.04 us -> 112 us
  matrix products: 101 us -> 0 us
  local copies, waits for them, and re-layouts: 74.8 us -> 23.4 us
  between operations: 13.4 us -> 0.26 us
  other arithmetic: 16.9 us -> 4.37 us
    all_gather x2 -> x0, waiting for transfers between devices: 499 us -> none  [the longest x1 326 us: body(): lax.all_gather(cycle_inter, 'col', axis=1, tiled=True)]
    all_to_all x2 -> x0, blocking collectives: 205 us -> none  [the longest x1 144 us: body(): lax.all_to_all(lax.all_to_all(doubles, 'row', split_axis=0, concat_axis=2...]
    ppermute x0 -> x29, waiting for transfers between devices: none -> 154 us  [the longest x13 96.3 us: send(): return lax.ppermute(x, 'col', pairs)]
    pallas_call x0 -> x16, Pallas kernels: none -> 142 us  [the longest x5 78.8 us: product(): pl.pallas_call(kernel, grid_spec=pltpu.PrefetchScalarGridSpec(num_scalar_...]
    ppermute x0 -> x29, starting transfers between devices: none -> 112 us  [the longest x13 99.6 us: send(): return lax.ppermute(x, 'col', pairs)]
    dot_general x1 -> x0, matrix products: 101 us -> none  [body(): jnp.dot(lax.all_gather(cycle_inter, 'col', axis=1, tiled=True), amp_panel...]
    all_to_all x5 -> x0, local copies, waits for them, and re-layouts: 33.4 us -> none  [the longest x4 32.6 us: body(): lax.all_to_all(doubles, 'row', split_axis=0, concat_axis=2, tiled=True)]
    all_to_all x1 -> x0, other arithmetic: 16.9 us -> none  [body(): lax.all_to_all(doubles, 'row', split_axis=0, concat_axis=2, tiled=True)]
  transfers between devices with their start and end apart: 2 -> 29, of which waited for: 2 -> 18; matrix products, arithmetic and copies ran while one was open for 0% -> 2% of each run, Pallas kernels for 0% -> 31%
where the time goes in v2:
time: 438 us; the launch traced here: 437 us
  waiting for transfers between devices  154 us (35%)
  Pallas kernels  142 us (32%)
  starting transfers between devices  112 us (26%)
  local copies, waits for them, and re-layouts  23.4 us (5%)
    ppermute x13, starting transfers between devices, send(): return lax.ppermute(x, 'col', pairs)  99.6 us
    ppermute x13, waiting for transfers between devices, send(): return lax.ppermute(x, 'col', pairs)  96.3 us
    pallas_call x5, Pallas kernels, product(): pl.pallas_call(kernel, grid_spec=pltpu.PrefetchScalarGridSpec(num_scalar_...  78.8 us
    ppermute x10, waiting for transfers between devices, across(): return lax.ppermute(x, 'row', [(a, a ^ bit) for a in range(rows_r)])  57.8 us
    pallas_call x4, Pallas kernels, panel(): pl.pallas_call(kernel, grid_spec=pltpu.PrefetchScalarGridSpec(num_scalar_...  41.4 us
    pallas_call x2, Pallas kernels, pack(): pl.pallas_call(kernel, grid_spec=pltpu.PrefetchScalarGridSpec(num_scalar_...  16.8 us
    unnamed x54, local copies, waits for them, and re-layouts  16.2 us
    ppermute x10, starting transfers between devices, across(): return lax.ppermute(x, 'row', [(a, a ^ bit) for a in range(rows_r)])  12.2 us
  transfers between devices with their start and end apart: 29, of which 18 were waited for; matrix products, arithmetic and copies ran while one was open for 2% of the time, Pallas kernels for 31%

profile of v2, /device:TPU:0, one launch (start us, length us, event | category | flops | bytes accessed | tf_op | source)
XLA Modules:
  0.0 436.7 jit_solution(2520017363514676427)
XLA Ops:
  2.0 7.8 %shard_map.37 = f32[4,192,768]{2,1,0:T(8,128)S(1)} custom-call(s32[16]{0:T(128)S(1)} %get-tuple-element.104.s_ref, f32[32,32,24,48]{3,2,1,0:T(8,128)} %bitcast.6), custom_call_target="tpu_custom_call" | custom-call | bytes 1440 | tf_op jit(solution)/shard_map/pallas_call | solution.py:78
  16.3 9.0 %shard_map.38 = (f32[2,192,768]{2,1,0:T(8,128)S(1)}, f32[2,192,768]{2,1,0:T(8,128)S(1)}, f32[2,192,768]{2,1,0:T(8,128)}, f32[2,192,768]{2,1,0:T(8,128)S(1)}) custom-call(s32[16]{0:T(128)S(1)} %get-tuple-element.105.s_ref, f32[32,32,24,48]{3,2,1,0:T(8,128)} %bitcast.7, f32[4,192,768]{2,1,0:T(8,128)S(1)} %collective-permute-done.got_ref), custom_call_target="tpu_custom_call" | custom-call | bytes 1440 | tf_op jit(solution)/shard_map/pallas_call | solution.py:78
  30.4 12.2 %collective-permute-start.5 = (f32[2,192,768]{2,1,0:T(8,128)S(1)}, f32[2,192,768]{2,1,0:T(8,128)S(1)}, u32[]{:S(2)}, u32[]{:S(2)}) collective-permute-start(f32[2,192,768]{2,1,0:T(8,128)S(1)} %get-tuple-element.55), channel_id=1, source_target_pairs={{2,0},{3,1},{0,2},{1,3},{6,4},{7,5},{4,6},{5,7},{10,8},{11,9},{8,1... | collective-permute-start | bytes 3538952 | tf_op jit(solution)/shard_map/ppermute | solution.py:263
  45.2 8.3 %collective-permute-done.6.refs_1_ = f32[2,192,768]{2,1,0:T(8,128)S(1)} collective-permute-done((f32[2,192,768]{2,1,0:T(8,128)S(1)}, f32[2,192,768]{2,1,0:T(8,128)S(1)}, u32[]{:S(2)}, u32[]{:S(2)}) %collective-permute-start.6) | collective-permute-done | bytes 1179680 | tf_op jit(solution)/shard_map/ppermute | solution.py:300
  55.7 13.4 %collective-permute-done.5.refs_0_ = f32[2,192,768]{2,1,0:T(8,128)S(1)} collective-permute-done((f32[2,192,768]{2,1,0:T(8,128)S(1)}, f32[2,192,768]{2,1,0:T(8,128)S(1)}, u32[]{:S(2)}, u32[]{:S(2)}) %collective-permute-start.5) | collective-permute-done | bytes 1179680 | tf_op jit(solution)/shard_map/ppermute | solution.py:263
  73.1 10.3 %collective-permute-done.2 = f32[192,768]{1,0:T(8,128)S(1)} collective-permute-done((f32[192,768]{1,0:T(8,128)S(1)}, f32[192,768]{1,0:T(8,128)S(1)}, u32[]{:S(2)}, u32[]{:S(2)}) %collective-permute-start.2) | collective-permute-done | bytes 589856 | tf_op jit(solution)/shard_map/ppermute | solution.py:263
  84.8 24.4 %collective-permute-done.7.refs_3_.refs_2_ = f32[3,192,768]{2,1,0:T(8,128)S(1)} collective-permute-done((f32[3,192,768]{2,1,0:T(8,128)S(1)}, f32[3,192,768]{2,1,0:T(8,128)S(1)}, u32[]{:S(2)}, u32[]{:S(2)}) %collective-permute-start.7) | collective-permute-done | bytes 1769504 | tf_op jit(solution)/shard_map/ppermute | solution.py:300
  117.2 22.4 %collective-permute-start.4 = (f32[2,192,768]{2,1,0:T(8,128)}, f32[2,192,768]{2,1,0:T(8,128)}, u32[]{:S(2)}, u32[]{:S(2)}) collective-permute-start(f32[2,192,768]{2,1,0:T(8,128)} %get-tuple-element.53), channel_id=1, source_target_pairs={{4,0},{5,1},{6,2},{7,3},{0,4},{1,5},{2,6},{3,7},{12,8},{13,9},{14,... | collective-permute-start | bytes 3538952 | tf_op jit(solution)/shard_map/ppermute | solution.py:263
  146.4 9.6 %shard_map.39 = (bf16[1536,3072]{1,0:T(8,128)(2,1)}, bf16[1536,3072]{1,0:T(8,128)(2,1)}) custom-call(s32[3]{0:T(128)S(1)} %pad_add_fusion.w_ref, f32[2,192,768]{2,1,0:T(8,128)S(1)} %copy-done.14, f32[2,192,768]{2,1,0:T(8,128)S(1)} %copy-done.10, f32[2,192,768]{2,1,0:T(8,128)S(1)} %copy-done.12, f32[3,192,768]{2,1,0:T(8,128)S(1)} %copy-done.1, ...), custom_call_target="tpu_custom_call" | custom-call | bytes 2304 | tf_op jit(solution)/shard_map/pallas_call | solution.py:132
  156.2 34.6 %collective-permute-done.4.refs_0_ = f32[2,192,768]{2,1,0:T(8,128)} collective-permute-done((f32[2,192,768]{2,1,0:T(8,128)}, f32[2,192,768]{2,1,0:T(8,128)}, u32[]{:S(2)}, u32[]{:S(2)}) %collective-permute-start.4) | collective-permute-done | bytes 1179680 | tf_op jit(solution)/shard_map/ppermute | solution.py:263
  199.8 9.7 %shard_map.40 = (bf16[1536,3072]{1,0:T(8,128)(2,1)}, bf16[1536,3072]{1,0:T(8,128)(2,1)}) custom-call(s32[3]{0:T(128)S(1)} %pad_add_fusion.w_ref, f32[2,192,768]{2,1,0:T(8,128)S(1)} %copy-done.6, f32[3,192,768]{2,1,0:T(8,128)S(1)} %copy-done.4, f32[3,192,768]{2,1,0:T(8,128)S(1)} %copy-done.2, ...), custom_call_target="tpu_custom_call", output_to_operand_aliasing={{0}: (6, {}), {1}: (7, {})} | custom-call | bytes 2304 | tf_op jit(solution)/shard_map/pallas_call | solution.py:132
  209.5 22.2 %collective-permute-done.14.refs_4_.refs_1_ = f32[3,192,768]{2,1,0:T(8,128)S(1)} collective-permute-done((f32[3,192,768]{2,1,0:T(8,128)S(1)}, f32[3,192,768]{2,1,0:T(8,128)S(1)}, u32[]{:S(2)}, u32[]{:S(2)}) %collective-permute-start.14) | collective-permute-done | bytes 1769504 | tf_op jit(solution)/shard_map/ppermute | solution.py:300
  234.1 9.6 %shard_map.41 = (bf16[1536,3072]{1,0:T(8,128)(2,1)}, bf16[1536,3072]{1,0:T(8,128)(2,1)}) custom-call(s32[3]{0:T(128)S(1)} %pad_add_fusion.w_ref, f32[2,192,768]{2,1,0:T(8,128)S(1)} %copy-done.8, f32[3,192,768]{2,1,0:T(8,128)S(1)} %collective-permute-done.8.refs_4_.refs_1_, ...), custom_call_target="tpu_custom_call", output_to_operand_aliasing={{0}: (6, {}), {1}: (7, {})} | custom-call | bytes 2304 | tf_op jit(solution)/shard_map/pallas_call | solution.py:132
  245.3 12.4 %shard_map.42 = (bf16[1536,3072]{1,0:T(8,128)(2,1)}, bf16[1536,3072]{1,0:T(8,128)(2,1)}) custom-call(s32[3]{0:T(128)S(1)} %pad_add_fusion.w_ref, f32[2,192,768]{2,1,0:T(8,128)} %collective-permute-done.4.refs_0_, f32[3,192,768]{2,1,0:T(8,128)S(1)} %collective-permute-done.14.refs_4_.refs_1_, ...), custom_call_target="tpu_custom_call", output_to_operand_aliasing={{0}: (6, {}), {1}: (7, {})} | custom-call | bytes 2304 | tf_op jit(solution)/shard_map/pallas_call | solution.py:132
  258.7 18.2 %shard_map.43 = (f32[384,768]{1,0:T(8,128)S(1)}, f32[384,768]{1,0:T(8,128)}) custom-call(s32[3]{0:T(128)S(1)} %pad_add_fusion.w_ref, f32[1536,768]{1,0:T(8,128)} %refs_0_.9, f32[384,768]{1,0:T(8,128)} %copy-done.17, f32[1536,768]{1,0:T(8,128)} %collective-permute-done.19.refs_2_, f32[384,768]{1,0:T(8,128)} %copy-done.19, ...), custom_call_target="tpu_custom_call" | custom-call | flops 2654208 | bytes 5760 | tf_op jit(solution)/shard_map/pallas_call | solution.py:193
  280.9 18.2 %shard_map.44 = (f32[384,768]{1,0:T(8,128)S(1)}, f32[384,768]{1,0:T(8,128)}) custom-call(s32[3]{0:T(128)S(1)} %pad_add_fusion.w_ref, f32[1536,768]{1,0:T(8,128)} %refs_0_.9, f32[384,768]{1,0:T(8,128)} %copy-done.18, f32[1536,768]{1,0:T(8,128)} %collective-permute-done.19.refs_2_, f32[384,768]{1,0:T(8,128)} %copy-done.22, ...), custom_call_target="tpu_custom_call" | custom-call | flops 2654208 | bytes 5760 | tf_op jit(solution)/shard_map/pallas_call | solution.py:193
  299.1 8.7 %collective-permute-done.17.refs_1_ = f32[384,768]{1,0:T(8,128)S(1)} collective-permute-done((f32[384,768]{1,0:T(8,128)S(1)}, f32[384,768]{1,0:T(8,128)S(1)}, u32[]{:S(2)}, u32[]{:S(2)}) %collective-permute-start.17) | collective-permute-done | bytes 1179680 | tf_op jit(solution)/shard_map/ppermute | solution.py:263
  310.3 20.5 %collective-permute-start.24 = (f32[384,768]{1,0:T(8,128)}, f32[384,768]{1,0:T(8,128)S(1)}, u32[]{:S(2)}, u32[]{:S(2)}) collective-permute-start(f32[384,768]{1,0:T(8,128)} %get-tuple-element.85), channel_id=1, source_target_pairs={{2,0},{3,1},{0,2},{1,3},{6,4},{7,5},{4,6},{5,7},{10,8},{11,9},{8,1... | collective-permute-start | bytes 3538952 | tf_op jit(solution)/shard_map/ppermute | solution.py:263
  334.2 18.2 %shard_map.45 = (f32[384,768]{1,0:T(8,128)S(1)}, f32[384,768]{1,0:T(8,128)}) custom-call(s32[3]{0:T(128)S(1)} %pad_add_fusion.w_ref, f32[1536,768]{1,0:T(8,128)} %refs_0_.9, f32[384,768]{1,0:T(8,128)} %copy-done.20, f32[1536,768]{1,0:T(8,128)} %collective-permute-done.19.refs_2_, f32[384,768]{1,0:T(8,128)} %copy-done.21, ...), custom_call_target="tpu_custom_call" | custom-call | flops 2654208 | bytes 5760 | tf_op jit(solution)/shard_map/pallas_call | solution.py:193
  358.4 25.4 %collective-permute-start.28 = (f32[384,768]{1,0:T(8,128)}, f32[384,768]{1,0:T(8,128)S(1)}, u32[]{:S(2)}, u32[]{:S(2)}) collective-permute-start(f32[384,768]{1,0:T(8,128)} %get-tuple-element.92), channel_id=1, source_target_pairs={{2,0},{3,1},{0,2},{1,3},{6,4},{7,5},{4,6},{5,7},{10,8},{11,9},{8,1... | collective-permute-start | bytes 3538952 | tf_op jit(solution)/shard_map/ppermute | solution.py:263
  384.8 12.1 %shard_map.46 = (f32[192,768]{1,0:T(8,128)S(1)}, f32[192,768]{1,0:T(8,128)S(1)}) custom-call(s32[3]{0:T(128)S(1)} %pad_add_fusion.w_ref, f32[1536,768]{1,0:T(8,128)} %refs_0_.9, f32[384,768]{1,0:T(8,128)} %copy-done.15, f32[1536,768]{1,0:T(8,128)} %collective-permute-done.19.refs_2_, f32[384,768]{1,0:T(8,128)} %copy-done.16, ...), custom_call_target="tpu_custom_call" | custom-call | flops 1327104 | bytes 5184 | tf_op jit(solution)/shard_map/pallas_call | solution.py:193
  399.8 12.1 %shard_map.47 = (f32[192,768]{1,0:T(8,128)S(1)}, f32[192,768]{1,0:T(8,128)S(1)}) custom-call(s32[3]{0:T(128)S(1)} %pad_add_fusion.w_ref, f32[1536,768]{1,0:T(8,128)} %refs_0_.9, f32[384,768]{1,0:T(8,128)} %copy-done.15, f32[1536,768]{1,0:T(8,128)} %collective-permute-done.19.refs_2_, f32[384,768]{1,0:T(8,128)} %copy-done.16, ...), custom_call_target="tpu_custom_call" | custom-call | flops 1327104 | bytes 5184 | tf_op jit(solution)/shard_map/pallas_call | solution.py:193
  415.2 8.3 %collective-permute-done.27.y_ref = f32[192,768]{1,0:T(8,128)S(1)} collective-permute-done((f32[192,768]{1,0:T(8,128)S(1)}, f32[192,768]{1,0:T(8,128)S(1)}, u32[]{:S(2)}, u32[]{:S(2)}) %collective-permute-start.27) | collective-permute-done | bytes 589856 | tf_op jit(solution)/shard_map/ppermute | solution.py:263
  424.3 11.5 %collective-permute-done.26.y_ref = f32[192,768]{1,0:T(8,128)S(1)} collective-permute-done((f32[192,768]{1,0:T(8,128)S(1)}, f32[192,768]{1,0:T(8,128)S(1)}, u32[]{:S(2)}, u32[]{:S(2)}) %collective-permute-start.26) | collective-permute-done | bytes 589856 | tf_op jit(solution)/shard_map/ppermute | solution.py:263
  (132 shorter events, 77.2 us)
Async XLA Ops:
  25.3 28.1 %collective-permute-start.6 = (f32[2,192,768]{2,1,0:T(8,128)S(1)}, f32[2,192,768]{2,1,0:T(8,128)S(1)}, u32[]{:S(2)}, u32[]{:S(2)}) collective-permute-start(f32[2,192,768]{2,1,0:T(8,128)S(1)} %get-tuple-element.56.refs_0_), channel_id=1, source_target_pairs={{0,8},{8,0},{16,24},{24,16},{1,9},{9,1},{17,25},{25,17},{2,10},{10... | collective-permute-start | bytes 3538952 | tf_op jit(solution)/shard_map/ppermute | solution.py:300
  26.8 27.8 %collective-permute-start.9 = (f32[2,192,768]{2,1,0:T(8,128)S(1)}, f32[2,192,768]{2,1,0:T(8,128)S(1)}, u32[]{:S(2)}, u32[]{:S(2)}) collective-permute-start(f32[2,192,768]{2,1,0:T(8,128)S(1)} %get-tuple-element.56.refs_0_), channel_id=1, source_target_pairs={{0,16},{8,24},{16,0},{24,8},{1,17},{9,25},{17,1},{25,9},{2,18},{10... | collective-permute-start | bytes 3538952 | tf_op jit(solution)/shard_map/ppermute | solution.py:300
  30.4 38.6 %collective-permute-start.5 = (f32[2,192,768]{2,1,0:T(8,128)S(1)}, f32[2,192,768]{2,1,0:T(8,128)S(1)}, u32[]{:S(2)}, u32[]{:S(2)}) collective-permute-start(f32[2,192,768]{2,1,0:T(8,128)S(1)} %get-tuple-element.55), channel_id=1, source_target_pairs={{2,0},{3,1},{0,2},{1,3},{6,4},{7,5},{4,6},{5,7},{10,8},{11,9},{8,1... | collective-permute-start | bytes 3538952 | tf_op jit(solution)/shard_map/ppermute | solution.py:263
  42.7 40.8 %collective-permute-start.2 = (f32[192,768]{1,0:T(8,128)S(1)}, f32[192,768]{1,0:T(8,128)S(1)}, u32[]{:S(2)}, u32[]{:S(2)}) collective-permute-start(f32[192,768]{1,0:T(8,128)S(1)} %get-tuple-element.51), channel_id=1, source_target_pairs={{6,0},{7,1},{4,2},{5,3},{2,4},{3,5},{0,6},{1,7},{14,8},{15,9},{12,... | collective-permute-start | bytes 1769480 | tf_op jit(solution)/shard_map/ppermute | solution.py:263
  70.1 39.1 %collective-permute-start.7 = (f32[3,192,768]{2,1,0:T(8,128)S(1)}, f32[3,192,768]{2,1,0:T(8,128)S(1)}, u32[]{:S(2)}, u32[]{:S(2)}) collective-permute-start(f32[3,192,768]{2,1,0:T(8,128)S(1)} %get-tuple-element.103), channel_id=1, source_target_pairs={{0,16},{8,24},{16,0},{24,8},{1,17},{9,25},{17,1},{25,9},{2,18},{10... | collective-permute-start | bytes 5308424 | tf_op jit(solution)/shard_map/ppermute | solution.py:300
  71.6 38.9 %collective-permute-start.10 = (f32[3,192,768]{2,1,0:T(8,128)S(1)}, f32[3,192,768]{2,1,0:T(8,128)S(1)}, u32[]{:S(2)}, u32[]{:S(2)}) collective-permute-start(f32[3,192,768]{2,1,0:T(8,128)S(1)} %get-tuple-element.102), channel_id=1, source_target_pairs={{0,8},{8,0},{16,24},{24,16},{1,9},{9,1},{17,25},{25,17},{2,10},{10... | collective-permute-start | bytes 5308424 | tf_op jit(solution)/shard_map/ppermute | solution.py:300
  83.5 28.5 %collective-permute-start.3 = (f32[2,192,768]{2,1,0:T(8,128)S(1)}, f32[2,192,768]{2,1,0:T(8,128)S(1)}, u32[]{:S(2)}, u32[]{:S(2)}) collective-permute-start(f32[2,192,768]{2,1,0:T(8,128)S(1)} %get-tuple-element.52), channel_id=1, source_target_pairs={{6,0},{7,1},{4,2},{5,3},{2,4},{3,5},{0,6},{1,7},{14,8},{15,9},{12,... | collective-permute-start | bytes 3538952 | tf_op jit(solution)/shard_map/ppermute | solution.py:263
  84.8 172.9 %collective-permute-start.19 = (f32[1536,768]{1,0:T(8,128)}, f32[1536,768]{1,0:T(8,128)}, u32[]{:S(2)}, u32[]{:S(2)}) collective-permute-start(f32[1536,768]{1,0:T(8,128)} %refs_0_.9), channel_id=1, source_target_pairs={{0,1},{1,0},{2,3},{3,2},{4,5},{5,4},{6,7},{7,6},{8,9},{9,8},{10,11... | collective-permute-start | bytes 14155784 | tf_op jit(solution)/shard_map/ppermute | solution.py:266
  114.2 41.9 %collective-permute-start.8 = (f32[3,192,768]{2,1,0:T(8,128)}, f32[3,192,768]{2,1,0:T(8,128)S(1)}, u32[]{:S(2)}, u32[]{:S(2)}) collective-permute-start(f32[3,192,768]{2,1,0:T(8,128)} %get-tuple-element.101), channel_id=1, source_target_pairs={{0,8},{8,0},{16,24},{24,16},{1,9},{9,1},{17,25},{25,17},{2,10},{10... | collective-permute-start | bytes 5308424 | tf_op jit(solution)/shard_map/ppermute | solution.py:300
  115.7 40.4 %collective-permute-start.12 = (f32[3,192,768]{2,1,0:T(8,128)}, f32[3,192,768]{2,1,0:T(8,128)S(1)}, u32[]{:S(2)}, u32[]{:S(2)}) collective-permute-start(f32[3,192,768]{2,1,0:T(8,128)} %get-tuple-element.100), channel_id=1, source_target_pairs={{0,16},{8,24},{16,0},{24,8},{1,17},{9,25},{17,1},{25,9},{2,18},{10... | collective-permute-start | bytes 5308424 | tf_op jit(solution)/shard_map/ppermute | solution.py:300
  117.2 73.5 %collective-permute-start.4 = (f32[2,192,768]{2,1,0:T(8,128)}, f32[2,192,768]{2,1,0:T(8,128)}, u32[]{:S(2)}, u32[]{:S(2)}) collective-permute-start(f32[2,192,768]{2,1,0:T(8,128)} %get-tuple-element.53), channel_id=1, source_target_pairs={{4,0},{5,1},{6,2},{7,3},{0,4},{1,5},{2,6},{3,7},{12,8},{13,9},{14,... | collective-permute-start | bytes 3538952 | tf_op jit(solution)/shard_map/ppermute | solution.py:263
  192.3 39.4 %collective-permute-start.14 = (f32[3,192,768]{2,1,0:T(8,128)S(1)}, f32[3,192,768]{2,1,0:T(8,128)S(1)}, u32[]{:S(2)}, u32[]{:S(2)}) collective-permute-start(f32[3,192,768]{2,1,0:T(8,128)S(1)} %get-tuple-element.63), channel_id=1, source_target_pairs={{0,8},{8,0},{16,24},{24,16},{1,9},{9,1},{17,25},{25,17},{2,10},{10... | collective-permute-start | bytes 5308424 | tf_op jit(solution)/shard_map/ppermute | solution.py:300
  192.9 39.1 %collective-permute-start.11 = (f32[3,192,768]{2,1,0:T(8,128)S(1)}, f32[3,192,768]{2,1,0:T(8,128)S(1)}, u32[]{:S(2)}, u32[]{:S(2)}) collective-permute-start(f32[3,192,768]{2,1,0:T(8,128)S(1)} %get-tuple-element.59), channel_id=1, source_target_pairs={{0,16},{8,24},{16,0},{24,8},{1,17},{9,25},{17,1},{25,9},{2,18},{10... | collective-permute-start | bytes 5308424 | tf_op jit(solution)/shard_map/ppermute | solution.py:300
  193.5 64.2 %collective-permute-start.20 = (f32[384,768]{1,0:T(8,128)S(1)}, f32[384,768]{1,0:T(8,128)S(1)}, u32[]{:S(2)}, u32[]{:S(2)}) collective-permute-start(f32[384,768]{1,0:T(8,128)S(1)} %pad_maximum_fusion.6.refs_1_), channel_id=1, source_target_pairs={{0,1},{1,0},{2,3},{3,2},{4,5},{5,4},{6,7},{7,6},{8,9},{9,8},{10,11... | collective-permute-start | bytes 3538952 | tf_op jit(solution)/shard_map/ppermute | solution.py:266
  197.3 79.6 %collective-permute-start.16 = (f32[384,768]{1,0:T(8,128)S(1)}, f32[384,768]{1,0:T(8,128)S(1)}, u32[]{:S(2)}, u32[]{:S(2)}) collective-permute-start(f32[384,768]{1,0:T(8,128)S(1)} %get-tuple-element.67), channel_id=1, source_target_pairs={{6,0},{7,1},{4,2},{5,3},{2,4},{3,5},{0,6},{1,7},{14,8},{15,9},{12,... | collective-permute-start | bytes 3538952 | tf_op jit(solution)/shard_map/ppermute | solution.py:263
  277.0 30.7 %collective-permute-start.17 = (f32[384,768]{1,0:T(8,128)S(1)}, f32[384,768]{1,0:T(8,128)S(1)}, u32[]{:S(2)}, u32[]{:S(2)}) collective-permute-start(f32[384,768]{1,0:T(8,128)S(1)} %get-tuple-element.68), channel_id=1, source_target_pairs={{6,0},{7,1},{4,2},{5,3},{2,4},{3,5},{0,6},{1,7},{14,8},{15,9},{12,... | collective-permute-start | bytes 3538952 | tf_op jit(solution)/shard_map/ppermute | solution.py:263
  279.7 53.5 %collective-permute-start.22 = (f32[384,768]{1,0:T(8,128)}, f32[384,768]{1,0:T(8,128)S(1)}, u32[]{:S(2)}, u32[]{:S(2)}) collective-permute-start(f32[384,768]{1,0:T(8,128)} %get-tuple-element.81), channel_id=1, source_target_pairs={{2,0},{3,1},{0,2},{1,3},{6,4},{7,5},{4,6},{5,7},{10,8},{11,9},{8,1... | collective-permute-start | bytes 3538952 | tf_op jit(solution)/shard_map/ppermute | solution.py:263
  307.8 25.4 %collective-permute-start.23 = (f32[384,768]{1,0:T(8,128)S(1)}, f32[384,768]{1,0:T(8,128)S(1)}, u32[]{:S(2)}, u32[]{:S(2)}) collective-permute-start(f32[384,768]{1,0:T(8,128)S(1)} %collective-permute-done.17.refs_1_), channel_id=1, source_target_pairs={{0,1},{1,0},{2,3},{3,2},{4,5},{5,4},{6,7},{7,6},{8,9},{9,8},{10,11... | collective-permute-start | bytes 3538952 | tf_op jit(solution)/shard_map/ppermute | solution.py:266
  307.8 50.6 %collective-permute-start.18 = (f32[384,768]{1,0:T(8,128)}, f32[384,768]{1,0:T(8,128)S(1)}, u32[]{:S(2)}, u32[]{:S(2)}) collective-permute-start(f32[384,768]{1,0:T(8,128)} %get-tuple-element.69), channel_id=1, source_target_pairs={{6,0},{7,1},{4,2},{5,3},{2,4},{3,5},{0,6},{1,7},{14,8},{15,9},{12,... | collective-permute-start | bytes 3538952 | tf_op jit(solution)/shard_map/ppermute | solution.py:263
  310.3 73.5 %collective-permute-start.24 = (f32[384,768]{1,0:T(8,128)}, f32[384,768]{1,0:T(8,128)S(1)}, u32[]{:S(2)}, u32[]{:S(2)}) collective-permute-start(f32[384,768]{1,0:T(8,128)} %get-tuple-element.85), channel_id=1, source_target_pairs={{2,0},{3,1},{0,2},{1,3},{6,4},{7,5},{4,6},{5,7},{10,8},{11,9},{8,1... | collective-permute-start | bytes 3538952 | tf_op jit(solution)/shard_map/ppermute | solution.py:263
  358.4 25.4 %collective-permute-start.25 = (f32[384,768]{1,0:T(8,128)S(1)}, f32[384,768]{1,0:T(8,128)S(1)}, u32[]{:S(2)}, u32[]{:S(2)}) collective-permute-start(f32[384,768]{1,0:T(8,128)S(1)} %collective-permute-done.18.refs_1_), channel_id=1, source_target_pairs={{0,1},{1,0},{2,3},{3,2},{4,5},{5,4},{6,7},{7,6},{8,9},{9,8},{10,11... | collective-permute-start | bytes 3538952 | tf_op jit(solution)/shard_map/ppermute | solution.py:266
  358.4 55.7 %collective-permute-start.28 = (f32[384,768]{1,0:T(8,128)}, f32[384,768]{1,0:T(8,128)S(1)}, u32[]{:S(2)}, u32[]{:S(2)}) collective-permute-start(f32[384,768]{1,0:T(8,128)} %get-tuple-element.92), channel_id=1, source_target_pairs={{2,0},{3,1},{0,2},{1,3},{6,4},{7,5},{4,6},{5,7},{10,8},{11,9},{8,1... | collective-permute-start | bytes 3538952 | tf_op jit(solution)/shard_map/ppermute | solution.py:263
  396.9 26.5 %collective-permute-start.27 = (f32[192,768]{1,0:T(8,128)S(1)}, f32[192,768]{1,0:T(8,128)S(1)}, u32[]{:S(2)}, u32[]{:S(2)}) collective-permute-start(f32[192,768]{1,0:T(8,128)S(1)} %get-tuple-element.91), channel_id=1, source_target_pairs={{2,0},{3,1},{0,2},{1,3},{6,4},{7,5},{4,6},{5,7},{10,8},{11,9},{8,1... | collective-permute-start | bytes 1769480 | tf_op jit(solution)/shard_map/ppermute | solution.py:263
  411.9 24.0 %collective-permute-start.26 = (f32[192,768]{1,0:T(8,128)S(1)}, f32[192,768]{1,0:T(8,128)S(1)}, u32[]{:S(2)}, u32[]{:S(2)}) collective-permute-start(f32[192,768]{1,0:T(8,128)S(1)} %get-tuple-element.90), channel_id=1, source_target_pairs={{2,0},{3,1},{0,2},{1,3},{6,4},{7,5},{4,6},{5,7},{10,8},{11,9},{8,1... | collective-permute-start | bytes 1769480 | tf_op jit(solution)/shard_map/ppermute | solution.py:263
  (32 other events, 259.2 us)

commit v3 on v2

--- a/solution.py
+++ b/solution.py
@@ -282,9 +282,6 @@
         x = cycle_inter[start : start + size]
         return [cross(after(x, *held), d) for d in offsets[1:]]
 
-    early = [take(0, eighth), take(eighth, sizes[0] - eighth)]
-    gathered = [[jnp.concatenate(x) for x in zip(*early)]]
-
     t = jnp.transpose(doubles, (0, 1, 3, 2))
     to = (p ^ jnp.arange(planes, dtype=jnp.int32))[:, None] ^ jnp.arange(2)
     to_kind = jnp.take(jnp.array(kind), jnp.repeat(to[:, 0], 2))
@@ -299,44 +296,57 @@
     def across(x, bit):
         return lax.ppermute(x, "row", [(a, a ^ bit) for a in range(rows_r)])
 
-    order = [0, 1] + list(range(planes - 1, 1, -1))
-    parts = [packed[0]] + [None] * (planes - 1)
+    order = [0, planes - 1] + list(range(1, planes - 1))
     links = [1 << i for i in range(rows_r.bit_length() - 1)]
-    brought, hilos, hilo = [], [], None
+    parts, brought, hilos, hilo = [packed[0]], [], [], None
+    first = {link: across(packed[0], link) for link in links}
+    brought.append(first)
+    firsts = {
+        link: across(first[links[1 - i]][1 - i : 2 - i], link)
+        for i, link in enumerate(links)
+    }
 
     def block(n, e):
         if e == 0:
             return [(parts[n], 0, 2)]
         if e in links:
             return [(brought[n][e], 0, 2)]
+        if n == 0:
+            return [(firsts[link], 0, 1) for link in links[::-1]]
         return [(brought[n + 1][link], 2 if n + 1 < planes else 0, 1) for link in links[::-1]]
 
-    for n in range(planes + 1):
+    def settle(n, hilo):
+        pieces = [block(n, e) for e in range(rows_r)]
+        return panel(where, order[n], pieces, hilo, planes, vb, k // planes, vr)
+
+    sent, early = {}, []
+    for n, d in enumerate(order[1:]):
+        if d == 1:
+            sent[d] = send(packed[d], [(q ^ d, q) for q in range(planes)])
+        else:
+            sent[d] = cross(packed[d], d)
+        if d != 1:
+            early.append(take(len(early) * eighth, eighth))
+    gathered = [[jnp.concatenate(x) for x in zip(*early)]]
+    for n in range(1, planes + 1):
         if n < planes:
-            d = order[n]
-            if n == 1:
-                x = after(packed[d], *early[0])
-                parts[n] = send(x, [(q ^ d, q) for q in range(planes)])
-            elif n:
-                parts[n] = cross(packed[d], d)
-            x = parts[n]
-        else:
-            gathered += [take(starts[1], sizes[1])]
-        held = hilos[n - 3] if n > 2 else ()
+            parts.append(sent[order[n]])
+        held = tuple(firsts.values()) if n < 3 else hilos[n - 3]
         now = {}
         for i, link in enumerate(links):
-            y = [x] if n < planes else []
-            if n:
+            y = [parts[n]] if n < planes else []
+            if n > 1:
                 y.append(brought[n - 1][links[1 - i]][1 - i : 2 - i])
             y = jnp.concatenate(y) if len(y) > 1 else y[0]
             now[link] = across(after(y, *held), link)
         brought.append(now)
-        if n:
-            pieces = [block(n - 1, e) for e in range(rows_r)]
-            hilo = panel(
-                where, order[n - 1], pieces, hilo, planes, vb, k // planes, vr
-            )
-            hilos.append(hilo)
+        if n == planes:
+            gathered += [take(starts[1], sizes[1])]
+        if n > 1:
+            hilo = settle(n - 1, hilo)
+        else:
+            hilo = settle(0, None)
+        hilos.append(hilo)
     last = brought[-1].values()
     gathered += [take(starts[i], sizes[i], *last) for i in range(2, len(sizes))]
 

time: 438 us -> 430 us (0.982)
  waiting for transfers between devices: 154 us -> 148 us
    ppermute x13, starting transfers between devices: 99.6 us -> 88.9 us  [send(): return lax.ppermute(x, 'col', pairs)]
    ppermute x13, waiting for transfers between devices: 96.3 us -> 89.6 us  [send(): return lax.ppermute(x, 'col', pairs)]
    ppermute x10 -> x12, starting transfers between devices: 12.2 us -> 18.5 us  [across(): return lax.ppermute(x, 'row', [(a, a ^ bit) for a in range(rows_r)])]
    ppermute x10 -> x12, waiting for transfers between devices: 57.8 us -> 54 us  [across(): return lax.ppermute(x, 'row', [(a, a ^ bit) for a in range(rows_r)])]
    unnamed x54 -> x56, local copies, waits for them, and re-layouts: 16.2 us -> 17.4 us
  transfers between devices with their start and end apart: 29 -> 31, of which waited for: 18 -> 20; matrix products, arithmetic and copies ran while one was open for 2% -> 3% of each run, Pallas kernels for 31% -> 29%
where the time goes in v3:
time: 430 us; the launch traced here: 429 us
  waiting for transfers between devices  148 us (34%)
  Pallas kernels  142 us (33%)
  starting transfers between devices  108 us (25%)
  local copies, waits for them, and re-layouts  25.4 us (6%)
  other arithmetic  5.25 us (1%)
    ppermute x13, waiting for transfers between devices, send(): return lax.ppermute(x, 'col', pairs)  89.6 us
    ppermute x13, starting transfers between devices, send(): return lax.ppermute(x, 'col', pairs)  88.9 us
    pallas_call x5, Pallas kernels, product(): pl.pallas_call(kernel, grid_spec=pltpu.PrefetchScalarGridSpec(num_scalar_...  79.6 us
    ppermute x12, waiting for transfers between devices, across(): return lax.ppermute(x, 'row', [(a, a ^ bit) for a in range(rows_r)])  54 us
    pallas_call x4, Pallas kernels, panel(): pl.pallas_call(kernel, grid_spec=pltpu.PrefetchScalarGridSpec(num_scalar_...  41.2 us
    ppermute x12, starting transfers between devices, across(): return lax.ppermute(x, 'row', [(a, a ^ bit) for a in range(rows_r)])  18.5 us
    unnamed x56, local copies, waits for them, and re-layouts  17.4 us
    pallas_call x2, Pallas kernels, pack(): pl.pallas_call(kernel, grid_spec=pltpu.PrefetchScalarGridSpec(num_scalar_...  16.8 us
  transfers between devices with their start and end apart: 31, of which 20 were waited for; matrix products, arithmetic and copies ran while one was open for 3% of the time, Pallas kernels for 29%

profile of v3, /device:TPU:0, one launch (start us, length us, event | category | flops | bytes accessed | tf_op | source)
XLA Modules:
  0.0 429.2 jit_solution(2182232338847013950)
XLA Ops:
  2.0 7.8 %shard_map.37 = f32[4,192,768]{2,1,0:T(8,128)S(1)} custom-call(s32[16]{0:T(128)S(1)} %get-tuple-element.106.s_ref, f32[32,32,24,48]{3,2,1,0:T(8,128)} %bitcast.6), custom_call_target="tpu_custom_call" | custom-call | bytes 1440 | tf_op jit(solution)/shard_map/pallas_call | solution.py:78
  14.5 9.0 %shard_map.38 = (f32[2,192,768]{2,1,0:T(8,128)S(1)}, f32[2,192,768]{2,1,0:T(8,128)S(1)}, f32[2,192,768]{2,1,0:T(8,128)}, f32[2,192,768]{2,1,0:T(8,128)S(1)}) custom-call(s32[16]{0:T(128)S(1)} %get-tuple-element.107.s_ref, f32[32,32,24,48]{3,2,1,0:T(8,128)} %bitcast.7, f32[4,192,768]{2,1,0:T(8,128)S(1)} %collective-permute-done.got_ref), custom_call_target="tpu_custom_call" | custom-call | bytes 1440 | tf_op jit(solution)/shard_map/pallas_call | solution.py:78
  32.5 20.1 %collective-permute-done.5.refs_2_ = f32[2,192,768]{2,1,0:T(8,128)S(1)} collective-permute-done((f32[2,192,768]{2,1,0:T(8,128)S(1)}, f32[2,192,768]{2,1,0:T(8,128)S(1)}, u32[]{:S(2)}, u32[]{:S(2)}) %collective-permute-start.5) | collective-permute-done | bytes 1179680 | tf_op jit(solution)/shard_map/ppermute | solution.py:297
  58.3 9.3 %collective-permute-done.6.refs_4_ = f32[1,192,768]{2,1,0:T(8,128)S(1)} collective-permute-done((f32[1,192,768]{2,1,0:T(8,128)S(1)}, f32[1,192,768]{2,1,0:T(8,128)S(1)}, u32[]{:S(2)}, u32[]{:S(2)}) %collective-permute-start.6) | collective-permute-done | bytes 589856 | tf_op jit(solution)/shard_map/ppermute | solution.py:297
  72.2 13.7 %collective-permute-start.4 = (f32[2,192,768]{2,1,0:T(8,128)S(1)}, f32[2,192,768]{2,1,0:T(8,128)S(1)}, u32[]{:S(2)}, u32[]{:S(2)}) collective-permute-start(f32[2,192,768]{2,1,0:T(8,128)S(1)} %get-tuple-element.55), channel_id=1, source_target_pairs={{2,0},{3,1},{0,2},{1,3},{6,4},{7,5},{4,6},{5,7},{10,8},{11,9},{8,1... | collective-permute-start | bytes 3538952 | tf_op jit(solution)/shard_map/ppermute | solution.py:263
  97.9 14.4 %collective-permute-done.4.refs_0_ = f32[2,192,768]{2,1,0:T(8,128)S(1)} collective-permute-done((f32[2,192,768]{2,1,0:T(8,128)S(1)}, f32[2,192,768]{2,1,0:T(8,128)S(1)}, u32[]{:S(2)}, u32[]{:S(2)}) %collective-permute-start.4) | collective-permute-done | bytes 1179680 | tf_op jit(solution)/shard_map/ppermute | solution.py:263
  117.7 7.4 %collective-permute-done.2 = f32[192,768]{1,0:T(8,128)} collective-permute-done((f32[192,768]{1,0:T(8,128)S(1)}, f32[192,768]{1,0:T(8,128)}, u32[]{:S(2)}, u32[]{:S(2)}) %collective-permute-start.2) | collective-permute-done | bytes 589856 | tf_op jit(solution)/shard_map/ppermute | solution.py:263
  131.1 9.3 %shard_map.39 = (bf16[1536,3072]{1,0:T(8,128)(2,1)S(1)}, bf16[1536,3072]{1,0:T(8,128)(2,1)}) custom-call(s32[3]{0:T(128)S(1)} %pad_add_fusion.w_ref, f32[2,192,768]{2,1,0:T(8,128)S(1)} %copy-done.14, f32[2,192,768]{2,1,0:T(8,128)S(1)} %copy-done.10, f32[2,192,768]{2,1,0:T(8,128)S(1)} %copy-done.8, f32[1,192,768]{2,1,0:T(8,128)S(1)} %copy-done.18, ...), custom_call_target="tpu_custom_call" | custom-call | bytes 2304 | tf_op jit(solution)/shard_map/pallas_call | solution.py:132
  144.1 7.5 %collective-permute-done.10.refs_4_.refs_1_ = f32[3,192,768]{2,1,0:T(8,128)S(1)} collective-permute-done((f32[3,192,768]{2,1,0:T(8,128)}, f32[3,192,768]{2,1,0:T(8,128)S(1)}, u32[]{:S(2)}, u32[]{:S(2)}) %collective-permute-start.10) | collective-permute-done | bytes 1769504 | tf_op jit(solution)/shard_map/ppermute | solution.py:297
  152.8 23.5 %collective-permute-done.3.refs_0_ = f32[2,192,768]{2,1,0:T(8,128)} collective-permute-done((f32[2,192,768]{2,1,0:T(8,128)}, f32[2,192,768]{2,1,0:T(8,128)}, u32[]{:S(2)}, u32[]{:S(2)}) %collective-permute-start.3) | collective-permute-done | bytes 1179680 | tf_op jit(solution)/shard_map/ppermute | solution.py:263
  182.5 15.0 %collective-permute-done.17 = f32[192,768]{1,0:T(8,128)S(1)} collective-permute-done((f32[192,768]{1,0:T(8,128)S(1)}, f32[192,768]{1,0:T(8,128)S(1)}, u32[]{:S(2)}, u32[]{:S(2)}) %collective-permute-start.17) | collective-permute-done | bytes 589856 | tf_op jit(solution)/shard_map/ppermute | solution.py:263
  204.1 9.8 %shard_map.40 = (bf16[1536,3072]{1,0:T(8,128)(2,1)}, bf16[1536,3072]{1,0:T(8,128)(2,1)}) custom-call(s32[3]{0:T(128)S(1)} %pad_add_fusion.w_ref, f32[2,192,768]{2,1,0:T(8,128)S(1)} %copy-done.12, f32[2,192,768]{2,1,0:T(8,128)S(1)} %copy-done.6, f32[2,192,768]{2,1,0:T(8,128)S(1)} %copy-done.4, ...), custom_call_target="tpu_custom_call", output_to_operand_aliasing={{0}: (6, {}), {1}: (7, {})} | custom-call | bytes 2304 | tf_op jit(solution)/shard_map/pallas_call | solution.py:132
  221.8 9.7 %shard_map.41 = (bf16[1536,3072]{1,0:T(8,128)(2,1)}, bf16[1536,3072]{1,0:T(8,128)(2,1)}) custom-call(s32[3]{0:T(128)S(1)} %pad_add_fusion.w_ref, f32[2,192,768]{2,1,0:T(8,128)S(1)} %copy-done.2, f32[3,192,768]{2,1,0:T(8,128)S(1)} %collective-permute-done.10.refs_4_.refs_1_, ...), custom_call_target="tpu_custom_call", output_to_operand_aliasing={{0}: (6, {}), {1}: (7, {})} | custom-call | bytes 2304 | tf_op jit(solution)/shard_map/pallas_call | solution.py:132
  235.1 12.4 %shard_map.42 = (bf16[1536,3072]{1,0:T(8,128)(2,1)}, bf16[1536,3072]{1,0:T(8,128)(2,1)}) custom-call(s32[3]{0:T(128)S(1)} %pad_add_fusion.w_ref, f32[2,192,768]{2,1,0:T(8,128)} %collective-permute-done.3.refs_0_, f32[3,192,768]{2,1,0:T(8,128)S(1)} %collective-permute-done.15.refs_4_.refs_1_, ...), custom_call_target="tpu_custom_call", output_to_operand_aliasing={{0}: (6, {}), {1}: (7, {})} | custom-call | bytes 2304 | tf_op jit(solution)/shard_map/pallas_call | solution.py:132
  248.5 18.6 %shard_map.43 = (f32[384,768]{1,0:T(8,128)S(1)}, f32[384,768]{1,0:T(8,128)}) custom-call(s32[3]{0:T(128)S(1)} %pad_add_fusion.w_ref, f32[1536,768]{1,0:T(8,128)} %refs_0_.9, f32[384,768]{1,0:T(8,128)} %copy-done.21, f32[1536,768]{1,0:T(8,128)} %collective-permute-done.21.refs_2_, f32[384,768]{1,0:T(8,128)} %copy-done.23, ...), custom_call_target="tpu_custom_call" | custom-call | flops 2654208 | bytes 5760 | tf_op jit(solution)/shard_map/pallas_call | solution.py:193
  268.5 27.5 %collective-permute-start.24 = (f32[384,768]{1,0:T(8,128)}, f32[384,768]{1,0:T(8,128)S(1)}, u32[]{:S(2)}, u32[]{:S(2)}) collective-permute-start(f32[384,768]{1,0:T(8,128)} %get-tuple-element.85), channel_id=1, source_target_pairs={{2,0},{3,1},{0,2},{1,3},{6,4},{7,5},{4,6},{5,7},{10,8},{11,9},{8,1... | collective-permute-start | bytes 3538952 | tf_op jit(solution)/shard_map/ppermute | solution.py:263
  297.0 18.3 %shard_map.44 = (f32[384,768]{1,0:T(8,128)S(1)}, f32[384,768]{1,0:T(8,128)}) custom-call(s32[3]{0:T(128)S(1)} %pad_add_fusion.w_ref, f32[1536,768]{1,0:T(8,128)} %refs_0_.9, f32[384,768]{1,0:T(8,128)} %copy-done.22, f32[1536,768]{1,0:T(8,128)} %collective-permute-done.21.refs_2_, f32[384,768]{1,0:T(8,128)} %copy-done.26, ...), custom_call_target="tpu_custom_call" | custom-call | flops 2654208 | bytes 5760 | tf_op jit(solution)/shard_map/pallas_call | solution.py:193
  325.6 18.4 %shard_map.45 = (f32[384,768]{1,0:T(8,128)S(1)}, f32[384,768]{1,0:T(8,128)}) custom-call(s32[3]{0:T(128)S(1)} %pad_add_fusion.w_ref, f32[1536,768]{1,0:T(8,128)} %refs_0_.9, f32[384,768]{1,0:T(8,128)} %copy-done.24, f32[1536,768]{1,0:T(8,128)} %collective-permute-done.21.refs_2_, f32[384,768]{1,0:T(8,128)} %copy-done.25, ...), custom_call_target="tpu_custom_call" | custom-call | flops 2654208 | bytes 5760 | tf_op jit(solution)/shard_map/pallas_call | solution.py:193
  344.0 7.2 %collective-permute-done.20.refs_1_ = f32[384,768]{1,0:T(8,128)S(1)} collective-permute-done((f32[384,768]{1,0:T(8,128)}, f32[384,768]{1,0:T(8,128)S(1)}, u32[]{:S(2)}, u32[]{:S(2)}) %collective-permute-start.20) | collective-permute-done | bytes 1179680 | tf_op jit(solution)/shard_map/ppermute | solution.py:263
  351.2 25.1 %collective-permute-start.30 = (f32[384,768]{1,0:T(8,128)}, f32[384,768]{1,0:T(8,128)S(1)}, u32[]{:S(2)}, u32[]{:S(2)}) collective-permute-start(f32[384,768]{1,0:T(8,128)} %get-tuple-element.96), channel_id=1, source_target_pairs={{2,0},{3,1},{0,2},{1,3},{6,4},{7,5},{4,6},{5,7},{10,8},{11,9},{8,1... | collective-permute-start | bytes 3538952 | tf_op jit(solution)/shard_map/ppermute | solution.py:263
  377.3 12.2 %shard_map.46 = (f32[192,768]{1,0:T(8,128)S(1)}, f32[192,768]{1,0:T(8,128)S(1)}) custom-call(s32[3]{0:T(128)S(1)} %pad_add_fusion.w_ref, f32[1536,768]{1,0:T(8,128)} %refs_0_.9, f32[384,768]{1,0:T(8,128)} %copy-done.19, f32[1536,768]{1,0:T(8,128)} %collective-permute-done.21.refs_2_, f32[384,768]{1,0:T(8,128)} %copy-done.20, ...), custom_call_target="tpu_custom_call" | custom-call | flops 1327104 | bytes 5184 | tf_op jit(solution)/shard_map/pallas_call | solution.py:193
  392.3 12.1 %shard_map.47 = (f32[192,768]{1,0:T(8,128)S(1)}, f32[192,768]{1,0:T(8,128)S(1)}) custom-call(s32[3]{0:T(128)S(1)} %pad_add_fusion.w_ref, f32[1536,768]{1,0:T(8,128)} %refs_0_.9, f32[384,768]{1,0:T(8,128)} %copy-done.19, f32[1536,768]{1,0:T(8,128)} %collective-permute-done.21.refs_2_, f32[384,768]{1,0:T(8,128)} %copy-done.20, ...), custom_call_target="tpu_custom_call" | custom-call | flops 1327104 | bytes 5184 | tf_op jit(solution)/shard_map/pallas_call | solution.py:193
  407.8 8.2 %collective-permute-done.29.y_ref = f32[192,768]{1,0:T(8,128)S(1)} collective-permute-done((f32[192,768]{1,0:T(8,128)S(1)}, f32[192,768]{1,0:T(8,128)S(1)}, u32[]{:S(2)}, u32[]{:S(2)}) %collective-permute-start.29) | collective-permute-done | bytes 589856 | tf_op jit(solution)/shard_map/ppermute | solution.py:263
  416.8 11.5 %collective-permute-done.28.y_ref = f32[192,768]{1,0:T(8,128)S(1)} collective-permute-done((f32[192,768]{1,0:T(8,128)S(1)}, f32[192,768]{1,0:T(8,128)S(1)}, u32[]{:S(2)}, u32[]{:S(2)}) %collective-permute-start.28) | collective-permute-done | bytes 589856 | tf_op jit(solution)/shard_map/ppermute | solution.py:263
  (137 shorter events, 100.8 us)
Async XLA Ops:
  23.4 29.2 %collective-permute-start.5 = (f32[2,192,768]{2,1,0:T(8,128)S(1)}, f32[2,192,768]{2,1,0:T(8,128)S(1)}, u32[]{:S(2)}, u32[]{:S(2)}) collective-permute-start(f32[2,192,768]{2,1,0:T(8,128)S(1)} %get-tuple-element.56.refs_0_), channel_id=1, source_target_pairs={{0,16},{8,24},{16,0},{24,8},{1,17},{9,25},{17,1},{25,9},{2,18},{10... | collective-permute-start | bytes 3538952 | tf_op jit(solution)/shard_map/ppermute | solution.py:297
  26.3 28.1 %collective-permute-start.7 = (f32[2,192,768]{2,1,0:T(8,128)S(1)}, f32[2,192,768]{2,1,0:T(8,128)S(1)}, u32[]{:S(2)}, u32[]{:S(2)}) collective-permute-start(f32[2,192,768]{2,1,0:T(8,128)S(1)} %get-tuple-element.56.refs_0_), channel_id=1, source_target_pairs={{0,8},{8,0},{16,24},{24,16},{1,9},{9,1},{17,25},{25,17},{2,10},{10... | collective-permute-start | bytes 3538952 | tf_op jit(solution)/shard_map/ppermute | solution.py:297
  28.9 29.4 %collective-permute-start.1 = (f32[2,192,768]{2,1,0:T(8,128)S(1)}, f32[2,192,768]{2,1,0:T(8,128)S(1)}, u32[]{:S(2)}, u32[]{:S(2)}) collective-permute-start(f32[2,192,768]{2,1,0:T(8,128)S(1)} %get-tuple-element.52), channel_id=1, source_target_pairs={{6,0},{7,1},{4,2},{5,3},{2,4},{3,5},{0,6},{1,7},{14,8},{15,9},{12,... | collective-permute-start | bytes 3538952 | tf_op jit(solution)/shard_map/ppermute | solution.py:263
  69.6 26.2 %collective-permute-start.9 = (f32[2,192,768]{2,1,0:T(8,128)S(1)}, f32[2,192,768]{2,1,0:T(8,128)S(1)}, u32[]{:S(2)}, u32[]{:S(2)}) collective-permute-start(f32[2,192,768]{2,1,0:T(8,128)S(1)} %collective-permute-done.1.refs_0_), channel_id=1, source_target_pairs={{0,16},{8,24},{16,0},{24,8},{1,17},{9,25},{17,1},{25,9},{2,18},{10... | collective-permute-start | bytes 3538952 | tf_op jit(solution)/shard_map/ppermute | solution.py:297
  71.2 25.7 %collective-permute-start.12 = (f32[2,192,768]{2,1,0:T(8,128)S(1)}, f32[2,192,768]{2,1,0:T(8,128)S(1)}, u32[]{:S(2)}, u32[]{:S(2)}) collective-permute-start(f32[2,192,768]{2,1,0:T(8,128)S(1)} %collective-permute-done.1.refs_0_), channel_id=1, source_target_pairs={{0,8},{8,0},{16,24},{24,16},{1,9},{9,1},{17,25},{25,17},{2,10},{10... | collective-permute-start | bytes 3538952 | tf_op jit(solution)/shard_map/ppermute | solution.py:297
  72.2 40.1 %collective-permute-start.4 = (f32[2,192,768]{2,1,0:T(8,128)S(1)}, f32[2,192,768]{2,1,0:T(8,128)S(1)}, u32[]{:S(2)}, u32[]{:S(2)}) collective-permute-start(f32[2,192,768]{2,1,0:T(8,128)S(1)} %get-tuple-element.55), channel_id=1, source_target_pairs={{2,0},{3,1},{0,2},{1,3},{6,4},{7,5},{4,6},{5,7},{10,8},{11,9},{8,1... | collective-permute-start | bytes 3538952 | tf_op jit(solution)/shard_map/ppermute | solution.py:263
  85.9 161.6 %collective-permute-start.21 = (f32[1536,768]{1,0:T(8,128)}, f32[1536,768]{1,0:T(8,128)}, u32[]{:S(2)}, u32[]{:S(2)}) collective-permute-start(f32[1536,768]{1,0:T(8,128)} %refs_0_.9), channel_id=1, source_target_pairs={{0,1},{1,0},{2,3},{3,2},{4,5},{5,4},{6,7},{7,6},{8,9},{9,8},{10,11... | collective-permute-start | bytes 14155784 | tf_op jit(solution)/shard_map/ppermute | solution.py:266
  88.1 37.0 %collective-permute-start.2 = (f32[192,768]{1,0:T(8,128)S(1)}, f32[192,768]{1,0:T(8,128)}, u32[]{:S(2)}, u32[]{:S(2)}) collective-permute-start(f32[192,768]{1,0:T(8,128)S(1)} %get-tuple-element.53), channel_id=1, source_target_pairs={{6,0},{7,1},{4,2},{5,3},{2,4},{3,5},{0,6},{1,7},{14,8},{15,9},{12,... | collective-permute-start | bytes 1769480 | tf_op jit(solution)/shard_map/ppermute | solution.py:263
  114.7 36.9 %collective-permute-start.10 = (f32[3,192,768]{2,1,0:T(8,128)}, f32[3,192,768]{2,1,0:T(8,128)S(1)}, u32[]{:S(2)}, u32[]{:S(2)}) collective-permute-start(f32[3,192,768]{2,1,0:T(8,128)} %get-tuple-element.58), channel_id=1, source_target_pairs={{0,8},{8,0},{16,24},{24,16},{1,9},{9,1},{17,25},{25,17},{2,10},{10... | collective-permute-start | bytes 5308424 | tf_op jit(solution)/shard_map/ppermute | solution.py:297
  116.1 36.6 %collective-permute-start.13 = (f32[3,192,768]{2,1,0:T(8,128)}, f32[3,192,768]{2,1,0:T(8,128)S(1)}, u32[]{:S(2)}, u32[]{:S(2)}) collective-permute-start(f32[3,192,768]{2,1,0:T(8,128)} %get-tuple-element.62), channel_id=1, source_target_pairs={{0,16},{8,24},{16,0},{24,8},{1,17},{9,25},{17,1},{25,9},{2,18},{10... | collective-permute-start | bytes 5308424 | tf_op jit(solution)/shard_map/ppermute | solution.py:297
  125.1 51.2 %collective-permute-start.3 = (f32[2,192,768]{2,1,0:T(8,128)}, f32[2,192,768]{2,1,0:T(8,128)}, u32[]{:S(2)}, u32[]{:S(2)}) collective-permute-start(f32[2,192,768]{2,1,0:T(8,128)} %get-tuple-element.54), channel_id=1, source_target_pairs={{4,0},{5,1},{6,2},{7,3},{0,4},{1,5},{2,6},{3,7},{12,8},{13,9},{14,... | collective-permute-start | bytes 3538952 | tf_op jit(solution)/shard_map/ppermute | solution.py:263
  177.9 40.6 %collective-permute-start.15 = (f32[3,192,768]{2,1,0:T(8,128)S(1)}, f32[3,192,768]{2,1,0:T(8,128)S(1)}, u32[]{:S(2)}, u32[]{:S(2)}) collective-permute-start(f32[3,192,768]{2,1,0:T(8,128)S(1)} %get-tuple-element.66), channel_id=1, source_target_pairs={{0,8},{8,0},{16,24},{24,16},{1,9},{9,1},{17,25},{25,17},{2,10},{10... | collective-permute-start | bytes 5308424 | tf_op jit(solution)/shard_map/ppermute | solution.py:297
  179.4 40.2 %collective-permute-start.11 = (f32[3,192,768]{2,1,0:T(8,128)S(1)}, f32[3,192,768]{2,1,0:T(8,128)S(1)}, u32[]{:S(2)}, u32[]{:S(2)}) collective-permute-start(f32[3,192,768]{2,1,0:T(8,128)S(1)} %get-tuple-element.61), channel_id=1, source_target_pairs={{0,16},{8,24},{16,0},{24,8},{1,17},{9,25},{17,1},{25,9},{2,18},{10... | collective-permute-start | bytes 5308424 | tf_op jit(solution)/shard_map/ppermute | solution.py:297
  198.7 48.8 %collective-permute-start.22 = (f32[384,768]{1,0:T(8,128)S(1)}, f32[384,768]{1,0:T(8,128)S(1)}, u32[]{:S(2)}, u32[]{:S(2)}) collective-permute-start(f32[384,768]{1,0:T(8,128)S(1)} %pad_maximum_fusion.4.refs_1_), channel_id=1, source_target_pairs={{0,1},{1,0},{2,3},{3,2},{4,5},{5,4},{6,7},{7,6},{8,9},{9,8},{10,11... | collective-permute-start | bytes 3538952 | tf_op jit(solution)/shard_map/ppermute | solution.py:266
  202.5 64.6 %collective-permute-start.18 = (f32[384,768]{1,0:T(8,128)S(1)}, f32[384,768]{1,0:T(8,128)S(1)}, u32[]{:S(2)}, u32[]{:S(2)}) collective-permute-start(f32[384,768]{1,0:T(8,128)S(1)} %get-tuple-element.71), channel_id=1, source_target_pairs={{6,0},{7,1},{4,2},{5,3},{2,4},{3,5},{0,6},{1,7},{14,8},{15,9},{12,... | collective-permute-start | bytes 3538952 | tf_op jit(solution)/shard_map/ppermute | solution.py:263
  267.1 28.9 %collective-permute-start.23 = (f32[384,768]{1,0:T(8,128)S(1)}, f32[384,768]{1,0:T(8,128)S(1)}, u32[]{:S(2)}, u32[]{:S(2)}) collective-permute-start(f32[384,768]{1,0:T(8,128)S(1)} %collective-permute-done.18.refs_1_), channel_id=1, source_target_pairs={{0,1},{1,0},{2,3},{3,2},{4,5},{5,4},{6,7},{7,6},{8,9},{9,8},{10,11... | collective-permute-start | bytes 3538952 | tf_op jit(solution)/shard_map/ppermute | solution.py:266
  267.2 48.1 %collective-permute-start.19 = (f32[384,768]{1,0:T(8,128)S(1)}, f32[384,768]{1,0:T(8,128)S(1)}, u32[]{:S(2)}, u32[]{:S(2)}) collective-permute-start(f32[384,768]{1,0:T(8,128)S(1)} %get-tuple-element.72), channel_id=1, source_target_pairs={{6,0},{7,1},{4,2},{5,3},{2,4},{3,5},{0,6},{1,7},{14,8},{15,9},{12,... | collective-permute-start | bytes 3538952 | tf_op jit(solution)/shard_map/ppermute | solution.py:263
  268.5 56.0 %collective-permute-start.24 = (f32[384,768]{1,0:T(8,128)}, f32[384,768]{1,0:T(8,128)S(1)}, u32[]{:S(2)}, u32[]{:S(2)}) collective-permute-start(f32[384,768]{1,0:T(8,128)} %get-tuple-element.85), channel_id=1, source_target_pairs={{2,0},{3,1},{0,2},{1,3},{6,4},{7,5},{4,6},{5,7},{10,8},{11,9},{8,1... | collective-permute-start | bytes 3538952 | tf_op jit(solution)/shard_map/ppermute | solution.py:263
  315.4 35.8 %collective-permute-start.20 = (f32[384,768]{1,0:T(8,128)}, f32[384,768]{1,0:T(8,128)S(1)}, u32[]{:S(2)}, u32[]{:S(2)}) collective-permute-start(f32[384,768]{1,0:T(8,128)} %get-tuple-element.73), channel_id=1, source_target_pairs={{6,0},{7,1},{4,2},{5,3},{2,4},{3,5},{0,6},{1,7},{14,8},{15,9},{12,... | collective-permute-start | bytes 3538952 | tf_op jit(solution)/shard_map/ppermute | solution.py:263
  318.2 58.1 %collective-permute-start.26 = (f32[384,768]{1,0:T(8,128)}, f32[384,768]{1,0:T(8,128)S(1)}, u32[]{:S(2)}, u32[]{:S(2)}) collective-permute-start(f32[384,768]{1,0:T(8,128)} %get-tuple-element.89), channel_id=1, source_target_pairs={{2,0},{3,1},{0,2},{1,3},{6,4},{7,5},{4,6},{5,7},{10,8},{11,9},{8,1... | collective-permute-start | bytes 3538952 | tf_op jit(solution)/shard_map/ppermute | solution.py:263
  351.2 25.1 %collective-permute-start.27 = (f32[384,768]{1,0:T(8,128)S(1)}, f32[384,768]{1,0:T(8,128)S(1)}, u32[]{:S(2)}, u32[]{:S(2)}) collective-permute-start(f32[384,768]{1,0:T(8,128)S(1)} %collective-permute-done.20.refs_1_), channel_id=1, source_target_pairs={{0,1},{1,0},{2,3},{3,2},{4,5},{5,4},{6,7},{7,6},{8,9},{9,8},{10,11... | collective-permute-start | bytes 3538952 | tf_op jit(solution)/shard_map/ppermute | solution.py:266
  351.2 55.5 %collective-permute-start.30 = (f32[384,768]{1,0:T(8,128)}, f32[384,768]{1,0:T(8,128)S(1)}, u32[]{:S(2)}, u32[]{:S(2)}) collective-permute-start(f32[384,768]{1,0:T(8,128)} %get-tuple-element.96), channel_id=1, source_target_pairs={{2,0},{3,1},{0,2},{1,3},{6,4},{7,5},{4,6},{5,7},{10,8},{11,9},{8,1... | collective-permute-start | bytes 3538952 | tf_op jit(solution)/shard_map/ppermute | solution.py:263
  389.5 26.5 %collective-permute-start.29 = (f32[192,768]{1,0:T(8,128)S(1)}, f32[192,768]{1,0:T(8,128)S(1)}, u32[]{:S(2)}, u32[]{:S(2)}) collective-permute-start(f32[192,768]{1,0:T(8,128)S(1)} %get-tuple-element.95), channel_id=1, source_target_pairs={{2,0},{3,1},{0,2},{1,3},{6,4},{7,5},{4,6},{5,7},{10,8},{11,9},{8,1... | collective-permute-start | bytes 1769480 | tf_op jit(solution)/shard_map/ppermute | solution.py:263
  404.5 23.9 %collective-permute-start.28 = (f32[192,768]{1,0:T(8,128)S(1)}, f32[192,768]{1,0:T(8,128)S(1)}, u32[]{:S(2)}, u32[]{:S(2)}) collective-permute-start(f32[192,768]{1,0:T(8,128)S(1)} %get-tuple-element.94), channel_id=1, source_target_pairs={{2,0},{3,1},{0,2},{1,3},{6,4},{7,5},{4,6},{5,7},{10,8},{11,9},{8,1... | collective-permute-start | bytes 1769480 | tf_op jit(solution)/shard_map/ppermute | solution.py:263
  (35 other events, 272.5 us)

commit v4 on v3

--- a/solution.py
+++ b/solution.py
@@ -151,10 +151,16 @@
     n //= 2
     per = len(offsets)
     tk = depth // (2 * per)
-    operands = own + other
+    pieces, places = [], []
+    for i, operand in enumerate(own + other):
+        at = 0
+        for piece in operand:
+            pieces.append(piece)
+            places.append((i, at, at + piece[2]))
+            at += piece[2]
 
     def kernel(w_ref, *refs):
-        ins, (h_ref, l_ref), outs = refs[: 2 * per], refs[2 * per : 2 * per + 2], refs[-3:-1]
+        ins, (h_ref, l_ref), outs = refs[:-5], refs[-5:-3], refs[-3:-1]
         x_ref = refs[-1]
         step = pl.program_id(0)
 
@@ -163,14 +169,16 @@
             for o in outs:
                 o[...] = jnp.zeros_like(o)
 
-        for i, ref in enumerate(ins):
+        for (i, at, end), ref in zip(places, ins):
 
             @pl.when(step == i)
             def _():
                 x = ref[...]
                 xh = x.astype(jnp.bfloat16)
-                x_ref[:m] = xh
-                x_ref[m:] = (x - xh.astype(jnp.float32)).astype(jnp.bfloat16)
+                x_ref[at:end] = xh
+                x_ref[m + at : m + end] = (x - xh.astype(jnp.float32)).astype(
+                    jnp.bfloat16
+                )
 
         dot = functools.partial(
             lax.dot_general, dimension_numbers=NT, preferred_element_type=jnp.float32
@@ -186,8 +194,8 @@
             plane = jnp.where(i % per == n, w[0] ^ offsets[n], plane)
         return 0, per * (w[1] ^ (i // per)) + plane // 2
 
-    def rows(chunk):
-        return pl.BlockSpec((m, tk), lambda i, w: (chunk, 0))
+    def rows(chunk, size):
+        return pl.BlockSpec((size, tk), lambda i, w: (chunk, 0))
 
     out = pl.BlockSpec((m, n), lambda i, w: (0, 0))
     return pl.pallas_call(
@@ -195,7 +203,7 @@
         grid_spec=pltpu.PrefetchScalarGridSpec(
             num_scalar_prefetch=1,
             grid=(2 * per,),
-            in_specs=[rows(c) for _, c in operands]
+            in_specs=[rows(c, size) for _, c, size in pieces]
             + [pl.BlockSpec((2 * n, tk), block)] * 2,
             out_specs=[out, out],
             scratch_shapes=[pltpu.VMEM((2 * m, tk), jnp.bfloat16)],
@@ -203,12 +211,11 @@
         out_shape=[jax.ShapeDtypeStruct((m, n), jnp.float32)] * 2,
         compiler_params=params(52),
         cost_estimate=cost(12 * m * n * depth, 4 * m * depth + 8 * n * depth),
-    )(where, *[x for x, _ in operands], hi, lo)
-
-
-def finish(x, y, into, start, m, rows):
-    n = x.shape[1]
-    tm = m // 2
+    )(where, *[x for x, _, _ in pieces], hi, lo)
+
+
+def finish(x, y, into, start, tm, rows):
+    m, n = x.shape
 
     def kernel(x_ref, y_ref, *refs):
         refs[-1][...] = x_ref[...] + y_ref[...]
@@ -221,7 +228,7 @@
         alias = {2: 0}
     return pl.pallas_call(
         kernel,
-        grid=(2,),
+        grid=(m // tm,),
         in_specs=specs,
         out_specs=pl.BlockSpec((tm, n), lambda i: (start // tm + i, 0)),
         out_shape=jax.ShapeDtypeStruct((rows, n), jnp.float32),
@@ -353,25 +360,22 @@
     result = None
     done, back = hilos[0][0], []
     own_other = swap(cycle_inter)
-    for i, came in enumerate(gathered):
+    for start, m, came in zip(starts, sizes, gathered):
         came = [after(x, done) for x in came]
         other = [swap(x) for x in came]
-        pieces = 1 if i + 1 < len(sizes) else 2
-        m = sizes[i] // pieces
-        for piece in range(pieces):
-            start = starts[i] + piece * m
-            came = [after(x, *back[: -1 - piece], done) for x in came]
-            mine, theirs = product(
-                where,
-                m,
-                offsets,
-                [(cycle_inter, start // m)] + [(x, piece) for x in came],
-                [(own_other, start // m)] + [(x, piece) for x in other],
-                hilo,
-            )
-            done = mine
-            back.append(send(theirs, [(q ^ 1, q) for q in range(planes)]))
-            result = finish(mine, back[-1], result, start, m, rows)
+        came = [after(x, *back[:-1], done) for x in came]
+        at = range(start // eighth, (start + m) // eighth)
+
+        def operands(whole, parts):
+            own = [(whole, n, eighth) for n in at]
+            return [own] + [[(x, 0, m)] for x in parts]
+
+        mine, theirs = product(
+            where, m, offsets, operands(cycle_inter, came), operands(own_other, other), hilo
+        )
+        done = mine
+        back.append(send(theirs, [(q ^ 1, q) for q in range(planes)]))
+        result = finish(mine, back[-1], result, start, eighth, rows)
     return result
 
 

time: 430 us -> 429 us (level)
  waiting for transfers between devices: 148 us -> 156 us
  Pallas kernels: 142 us -> 135 us
    ppermute x13 -> x12, waiting for transfers between devices: 89.6 us -> 96.3 us  [send(): return lax.ppermute(x, 'col', pairs)]
    pallas_call x5 -> x4, Pallas kernels: 79.6 us -> 73.3 us  [product(): pl.pallas_call(kernel, grid_spec=pltpu.PrefetchScalarGridSpec(num_scalar_...]
    ppermute x13 -> x12, starting transfers between devices: 88.9 us -> 88.2 us  [send(): return lax.ppermute(x, 'col', pairs)]
  transfers between devices with their start and end apart: 31 -> 30, of which waited for: 20 -> 20; matrix products, arithmetic and copies ran while one was open for 3% -> 2% of each run, Pallas kernels for 29% -> 27%
where the time goes in v4:
time: 429 us; the launch traced here: 428 us
  waiting for transfers between devices  156 us (36%)
  Pallas kernels  135 us (31%)
  starting transfers between devices  107 us (25%)
  local copies, waits for them, and re-layouts  24.4 us (6%)
  other arithmetic  5.22 us (1%)
    ppermute x12, waiting for transfers between devices, send(): return lax.ppermute(x, 'col', pairs)  96.3 us
    ppermute x12, starting transfers between devices, send(): return lax.ppermute(x, 'col', pairs)  88.2 us
    pallas_call x4, Pallas kernels, product(): pl.pallas_call(kernel, grid_spec=pltpu.PrefetchScalarGridSpec(num_scalar_...  73.3 us
    ppermute x12, waiting for transfers between devices, across(): return lax.ppermute(x, 'row', [(a, a ^ bit) for a in range(rows_r)])  55.1 us
    pallas_call x4, Pallas kernels, panel(): pl.pallas_call(kernel, grid_spec=pltpu.PrefetchScalarGridSpec(num_scalar_...  41 us
    ppermute x12, starting transfers between devices, across(): return lax.ppermute(x, 'row', [(a, a ^ bit) for a in range(rows_r)])  18.5 us
    unnamed x56, local copies, waits for them, and re-layouts  17.4 us
    pallas_call x2, Pallas kernels, pack(): pl.pallas_call(kernel, grid_spec=pltpu.PrefetchScalarGridSpec(num_scalar_...  16.8 us
  transfers between devices with their start and end apart: 30, of which 20 were waited for; matrix products, arithmetic and copies ran while one was open for 2% of the time, Pallas kernels for 27%

profile of v4, /device:TPU:0, one launch (start us, length us, event | category | flops | bytes accessed | tf_op | source)
XLA Modules:
  0.0 428.2 jit_solution(1855259994172862526)
XLA Ops:
  2.0 7.8 %shard_map.37 = f32[4,192,768]{2,1,0:T(8,128)S(1)} custom-call(s32[16]{0:T(128)S(1)} %get-tuple-element.100.s_ref, f32[32,32,24,48]{3,2,1,0:T(8,128)} %bitcast.6), custom_call_target="tpu_custom_call" | custom-call | bytes 1440 | tf_op jit(solution)/shard_map/pallas_call | solution.py:78
  14.5 9.0 %shard_map.38 = (f32[2,192,768]{2,1,0:T(8,128)S(1)}, f32[2,192,768]{2,1,0:T(8,128)S(1)}, f32[2,192,768]{2,1,0:T(8,128)}, f32[2,192,768]{2,1,0:T(8,128)S(1)}) custom-call(s32[16]{0:T(128)S(1)} %get-tuple-element.101.s_ref, f32[32,32,24,48]{3,2,1,0:T(8,128)} %bitcast.7, f32[4,192,768]{2,1,0:T(8,128)S(1)} %collective-permute-done.got_ref), custom_call_target="tpu_custom_call" | custom-call | bytes 1440 | tf_op jit(solution)/shard_map/pallas_call | solution.py:78
  32.5 20.1 %collective-permute-done.5.refs_2_ = f32[2,192,768]{2,1,0:T(8,128)S(1)} collective-permute-done((f32[2,192,768]{2,1,0:T(8,128)S(1)}, f32[2,192,768]{2,1,0:T(8,128)S(1)}, u32[]{:S(2)}, u32[]{:S(2)}) %collective-permute-start.5) | collective-permute-done | bytes 1179680 | tf_op jit(solution)/shard_map/ppermute | solution.py:304
  58.3 9.3 %collective-permute-done.6.refs_4_ = f32[1,192,768]{2,1,0:T(8,128)S(1)} collective-permute-done((f32[1,192,768]{2,1,0:T(8,128)S(1)}, f32[1,192,768]{2,1,0:T(8,128)S(1)}, u32[]{:S(2)}, u32[]{:S(2)}) %collective-permute-start.6) | collective-permute-done | bytes 589856 | tf_op jit(solution)/shard_map/ppermute | solution.py:304
  72.2 13.7 %collective-permute-start.4 = (f32[2,192,768]{2,1,0:T(8,128)S(1)}, f32[2,192,768]{2,1,0:T(8,128)S(1)}, u32[]{:S(2)}, u32[]{:S(2)}) collective-permute-start(f32[2,192,768]{2,1,0:T(8,128)S(1)} %get-tuple-element.52), channel_id=1, source_target_pairs={{2,0},{3,1},{0,2},{1,3},{6,4},{7,5},{4,6},{5,7},{10,8},{11,9},{8,1... | collective-permute-start | bytes 3538952 | tf_op jit(solution)/shard_map/ppermute | solution.py:270
  97.9 14.4 %collective-permute-done.4.refs_0_ = f32[2,192,768]{2,1,0:T(8,128)S(1)} collective-permute-done((f32[2,192,768]{2,1,0:T(8,128)S(1)}, f32[2,192,768]{2,1,0:T(8,128)S(1)}, u32[]{:S(2)}, u32[]{:S(2)}) %collective-permute-start.4) | collective-permute-done | bytes 1179680 | tf_op jit(solution)/shard_map/ppermute | solution.py:270
  117.7 7.5 %collective-permute-done.2 = f32[192,768]{1,0:T(8,128)} collective-permute-done((f32[192,768]{1,0:T(8,128)S(1)}, f32[192,768]{1,0:T(8,128)}, u32[]{:S(2)}, u32[]{:S(2)}) %collective-permute-start.2) | collective-permute-done | bytes 589856 | tf_op jit(solution)/shard_map/ppermute | solution.py:270
  131.1 9.3 %shard_map.39 = (bf16[1536,3072]{1,0:T(8,128)(2,1)S(1)}, bf16[1536,3072]{1,0:T(8,128)(2,1)}) custom-call(s32[3]{0:T(128)S(1)} %pad_add_fusion.w_ref, f32[2,192,768]{2,1,0:T(8,128)S(1)} %copy-done.14, f32[2,192,768]{2,1,0:T(8,128)S(1)} %copy-done.10, f32[2,192,768]{2,1,0:T(8,128)S(1)} %copy-done.8, f32[1,192,768]{2,1,0:T(8,128)S(1)} %copy-done.18, ...), custom_call_target="tpu_custom_call" | custom-call | bytes 2304 | tf_op jit(solution)/shard_map/pallas_call | solution.py:132
  144.0 7.5 %collective-permute-done.10.refs_4_.refs_1_ = f32[3,192,768]{2,1,0:T(8,128)S(1)} collective-permute-done((f32[3,192,768]{2,1,0:T(8,128)}, f32[3,192,768]{2,1,0:T(8,128)S(1)}, u32[]{:S(2)}, u32[]{:S(2)}) %collective-permute-start.10) | collective-permute-done | bytes 1769504 | tf_op jit(solution)/shard_map/ppermute | solution.py:304
  152.8 23.5 %collective-permute-done.3.refs_0_ = f32[2,192,768]{2,1,0:T(8,128)} collective-permute-done((f32[2,192,768]{2,1,0:T(8,128)}, f32[2,192,768]{2,1,0:T(8,128)}, u32[]{:S(2)}, u32[]{:S(2)}) %collective-permute-start.3) | collective-permute-done | bytes 1179680 | tf_op jit(solution)/shard_map/ppermute | solution.py:270
  182.5 15.0 %collective-permute-done.17 = f32[192,768]{1,0:T(8,128)S(1)} collective-permute-done((f32[192,768]{1,0:T(8,128)S(1)}, f32[192,768]{1,0:T(8,128)S(1)}, u32[]{:S(2)}, u32[]{:S(2)}) %collective-permute-start.17) | collective-permute-done | bytes 589856 | tf_op jit(solution)/shard_map/ppermute | solution.py:270
  203.2 9.7 %shard_map.40 = (bf16[1536,3072]{1,0:T(8,128)(2,1)}, bf16[1536,3072]{1,0:T(8,128)(2,1)}) custom-call(s32[3]{0:T(128)S(1)} %pad_add_fusion.w_ref, f32[2,192,768]{2,1,0:T(8,128)S(1)} %copy-done.12, f32[2,192,768]{2,1,0:T(8,128)S(1)} %copy-done.6, f32[2,192,768]{2,1,0:T(8,128)S(1)} %copy-done.4, ...), custom_call_target="tpu_custom_call", output_to_operand_aliasing={{0}: (6, {}), {1}: (7, {})} | custom-call | bytes 2304 | tf_op jit(solution)/shard_map/pallas_call | solution.py:132
  212.8 5.6 %collective-permute-done.15.refs_4_.refs_1_ = f32[3,192,768]{2,1,0:T(8,128)S(1)} collective-permute-done((f32[3,192,768]{2,1,0:T(8,128)S(1)}, f32[3,192,768]{2,1,0:T(8,128)S(1)}, u32[]{:S(2)}, u32[]{:S(2)}) %collective-permute-start.15) | collective-permute-done | bytes 1769504 | tf_op jit(solution)/shard_map/ppermute | solution.py:304
  221.8 9.7 %shard_map.41 = (bf16[1536,3072]{1,0:T(8,128)(2,1)}, bf16[1536,3072]{1,0:T(8,128)(2,1)}) custom-call(s32[3]{0:T(128)S(1)} %pad_add_fusion.w_ref, f32[2,192,768]{2,1,0:T(8,128)S(1)} %copy-done.2, f32[3,192,768]{2,1,0:T(8,128)S(1)} %collective-permute-done.10.refs_4_.refs_1_, ...), custom_call_target="tpu_custom_call", output_to_operand_aliasing={{0}: (6, {}), {1}: (7, {})} | custom-call | bytes 2304 | tf_op jit(solution)/shard_map/pallas_call | solution.py:132
  235.1 12.4 %shard_map.42 = (bf16[1536,3072]{1,0:T(8,128)(2,1)}, bf16[1536,3072]{1,0:T(8,128)(2,1)}) custom-call(s32[3]{0:T(128)S(1)} %pad_add_fusion.w_ref, f32[2,192,768]{2,1,0:T(8,128)} %collective-permute-done.3.refs_0_, f32[3,192,768]{2,1,0:T(8,128)S(1)} %collective-permute-done.15.refs_4_.refs_1_, ...), custom_call_target="tpu_custom_call", output_to_operand_aliasing={{0}: (6, {}), {1}: (7, {})} | custom-call | bytes 2304 | tf_op jit(solution)/shard_map/pallas_call | solution.py:132
  248.5 18.3 %shard_map.43 = (f32[384,768]{1,0:T(8,128)S(1)}, f32[384,768]{1,0:T(8,128)}) custom-call(s32[3]{0:T(128)S(1)} %pad_add_fusion.w_ref, f32[1536,768]{1,0:T(8,128)} %refs_1_.7, f32[1536,768]{1,0:T(8,128)} %refs_1_.7, f32[384,768]{1,0:T(8,128)} %copy-done.19, f32[1536,768]{1,0:T(8,128)} %collective-permute-done.21.refs_3_.refs_4_, ...), custom_call_target="tpu_custom_call" | custom-call | flops 2654208 | bytes 5760 | tf_op jit(solution)/shard_map/pallas_call | solution.py:201
  268.6 26.8 %collective-permute-start.24 = (f32[384,768]{1,0:T(8,128)}, f32[384,768]{1,0:T(8,128)S(1)}, u32[]{:S(2)}, u32[]{:S(2)}) collective-permute-start(f32[384,768]{1,0:T(8,128)} %get-tuple-element.82), channel_id=1, source_target_pairs={{2,0},{3,1},{0,2},{1,3},{6,4},{7,5},{4,6},{5,7},{10,8},{11,9},{8,1... | collective-permute-start | bytes 3538952 | tf_op jit(solution)/shard_map/ppermute | solution.py:270
  296.5 18.4 %shard_map.44 = (f32[384,768]{1,0:T(8,128)S(1)}, f32[384,768]{1,0:T(8,128)}) custom-call(s32[3]{0:T(128)S(1)} %pad_add_fusion.w_ref, f32[1536,768]{1,0:T(8,128)} %refs_1_.7, f32[1536,768]{1,0:T(8,128)} %refs_1_.7, f32[384,768]{1,0:T(8,128)} %copy-done.20, f32[1536,768]{1,0:T(8,128)} %collective-permute-done.21.refs_3_.refs_4_, ...), custom_call_target="tpu_custom_call" | custom-call | flops 2654208 | bytes 5760 | tf_op jit(solution)/shard_map/pallas_call | solution.py:201
  317.4 6.4 %collective-permute-start.26 = (f32[384,768]{1,0:T(8,128)}, f32[384,768]{1,0:T(8,128)S(1)}, u32[]{:S(2)}, u32[]{:S(2)}) collective-permute-start(f32[384,768]{1,0:T(8,128)} %get-tuple-element.86), channel_id=1, source_target_pairs={{2,0},{3,1},{0,2},{1,3},{6,4},{7,5},{4,6},{5,7},{10,8},{11,9},{8,1... | collective-permute-start | bytes 3538952 | tf_op jit(solution)/shard_map/ppermute | solution.py:270
  324.8 18.3 %shard_map.45 = (f32[384,768]{1,0:T(8,128)S(1)}, f32[384,768]{1,0:T(8,128)}) custom-call(s32[3]{0:T(128)S(1)} %pad_add_fusion.w_ref, f32[1536,768]{1,0:T(8,128)} %refs_1_.7, f32[1536,768]{1,0:T(8,128)} %refs_1_.7, f32[384,768]{1,0:T(8,128)} %copy-done.23, f32[1536,768]{1,0:T(8,128)} %collective-permute-done.21.refs_3_.refs_4_, ...), custom_call_target="tpu_custom_call" | custom-call | flops 2654208 | bytes 5760 | tf_op jit(solution)/shard_map/pallas_call | solution.py:201
  343.1 6.8 %collective-permute-done.20.refs_2_ = f32[384,768]{1,0:T(8,128)S(1)} collective-permute-done((f32[384,768]{1,0:T(8,128)S(1)}, f32[384,768]{1,0:T(8,128)S(1)}, u32[]{:S(2)}, u32[]{:S(2)}) %collective-permute-start.20) | collective-permute-done | bytes 1179680 | tf_op jit(solution)/shard_map/ppermute | solution.py:270
  350.0 25.1 %collective-permute-start.29 = (f32[384,768]{1,0:T(8,128)}, f32[384,768]{1,0:T(8,128)S(1)}, u32[]{:S(2)}, u32[]{:S(2)}) collective-permute-start(f32[384,768]{1,0:T(8,128)} %get-tuple-element.90), channel_id=1, source_target_pairs={{2,0},{3,1},{0,2},{1,3},{6,4},{7,5},{4,6},{5,7},{10,8},{11,9},{8,1... | collective-permute-start | bytes 3538952 | tf_op jit(solution)/shard_map/ppermute | solution.py:270
  376.1 18.3 %shard_map.46 = (f32[384,768]{1,0:T(8,128)S(1)}, f32[384,768]{1,0:T(8,128)}) custom-call(s32[3]{0:T(128)S(1)} %pad_add_fusion.w_ref, f32[1536,768]{1,0:T(8,128)} %refs_1_.7, f32[1536,768]{1,0:T(8,128)} %refs_1_.7, f32[384,768]{1,0:T(8,128)} %copy-done.22, f32[1536,768]{1,0:T(8,128)} %collective-permute-done.21.refs_3_.refs_4_, ...), custom_call_target="tpu_custom_call" | custom-call | flops 2654208 | bytes 5760 | tf_op jit(solution)/shard_map/pallas_call | solution.py:201
  403.2 24.0 %collective-permute-done.28.y_ref = f32[384,768]{1,0:T(8,128)S(1)} collective-permute-done((f32[384,768]{1,0:T(8,128)}, f32[384,768]{1,0:T(8,128)S(1)}, u32[]{:S(2)}, u32[]{:S(2)}) %collective-permute-start.28) | collective-permute-done | bytes 1179680 | tf_op jit(solution)/shard_map/ppermute | solution.py:270
  (133 shorter events, 91.0 us)
Async XLA Ops:
  23.4 29.2 %collective-permute-start.5 = (f32[2,192,768]{2,1,0:T(8,128)S(1)}, f32[2,192,768]{2,1,0:T(8,128)S(1)}, u32[]{:S(2)}, u32[]{:S(2)}) collective-permute-start(f32[2,192,768]{2,1,0:T(8,128)S(1)} %get-tuple-element.53.refs_0_), channel_id=1, source_target_pairs={{0,16},{8,24},{16,0},{24,8},{1,17},{9,25},{17,1},{25,9},{2,18},{10... | collective-permute-start | bytes 3538952 | tf_op jit(solution)/shard_map/ppermute | solution.py:304
  26.3 28.1 %collective-permute-start.7 = (f32[2,192,768]{2,1,0:T(8,128)S(1)}, f32[2,192,768]{2,1,0:T(8,128)S(1)}, u32[]{:S(2)}, u32[]{:S(2)}) collective-permute-start(f32[2,192,768]{2,1,0:T(8,128)S(1)} %get-tuple-element.53.refs_0_), channel_id=1, source_target_pairs={{0,8},{8,0},{16,24},{24,16},{1,9},{9,1},{17,25},{25,17},{2,10},{10... | collective-permute-start | bytes 3538952 | tf_op jit(solution)/shard_map/ppermute | solution.py:304
  28.9 29.4 %collective-permute-start.1 = (f32[2,192,768]{2,1,0:T(8,128)S(1)}, f32[2,192,768]{2,1,0:T(8,128)S(1)}, u32[]{:S(2)}, u32[]{:S(2)}) collective-permute-start(f32[2,192,768]{2,1,0:T(8,128)S(1)} %get-tuple-element.49), channel_id=1, source_target_pairs={{6,0},{7,1},{4,2},{5,3},{2,4},{3,5},{0,6},{1,7},{14,8},{15,9},{12,... | collective-permute-start | bytes 3538952 | tf_op jit(solution)/shard_map/ppermute | solution.py:270
  69.7 26.2 %collective-permute-start.9 = (f32[2,192,768]{2,1,0:T(8,128)S(1)}, f32[2,192,768]{2,1,0:T(8,128)S(1)}, u32[]{:S(2)}, u32[]{:S(2)}) collective-permute-start(f32[2,192,768]{2,1,0:T(8,128)S(1)} %collective-permute-done.1.refs_0_), channel_id=1, source_target_pairs={{0,16},{8,24},{16,0},{24,8},{1,17},{9,25},{17,1},{25,9},{2,18},{10... | collective-permute-start | bytes 3538952 | tf_op jit(solution)/shard_map/ppermute | solution.py:304
  71.2 25.7 %collective-permute-start.12 = (f32[2,192,768]{2,1,0:T(8,128)S(1)}, f32[2,192,768]{2,1,0:T(8,128)S(1)}, u32[]{:S(2)}, u32[]{:S(2)}) collective-permute-start(f32[2,192,768]{2,1,0:T(8,128)S(1)} %collective-permute-done.1.refs_0_), channel_id=1, source_target_pairs={{0,8},{8,0},{16,24},{24,16},{1,9},{9,1},{17,25},{25,17},{2,10},{10... | collective-permute-start | bytes 3538952 | tf_op jit(solution)/shard_map/ppermute | solution.py:304
  72.2 40.1 %collective-permute-start.4 = (f32[2,192,768]{2,1,0:T(8,128)S(1)}, f32[2,192,768]{2,1,0:T(8,128)S(1)}, u32[]{:S(2)}, u32[]{:S(2)}) collective-permute-start(f32[2,192,768]{2,1,0:T(8,128)S(1)} %get-tuple-element.52), channel_id=1, source_target_pairs={{2,0},{3,1},{0,2},{1,3},{6,4},{7,5},{4,6},{5,7},{10,8},{11,9},{8,1... | collective-permute-start | bytes 3538952 | tf_op jit(solution)/shard_map/ppermute | solution.py:270
  86.0 161.6 %collective-permute-start.21 = (f32[1536,768]{1,0:T(8,128)}, f32[1536,768]{1,0:T(8,128)}, u32[]{:S(2)}, u32[]{:S(2)}) collective-permute-start(f32[1536,768]{1,0:T(8,128)} %refs_1_.7), channel_id=1, source_target_pairs={{0,1},{1,0},{2,3},{3,2},{4,5},{5,4},{6,7},{7,6},{8,9},{9,8},{10,11... | collective-permute-start | bytes 14155784 | tf_op jit(solution)/shard_map/ppermute | solution.py:273
  88.1 37.0 %collective-permute-start.2 = (f32[192,768]{1,0:T(8,128)S(1)}, f32[192,768]{1,0:T(8,128)}, u32[]{:S(2)}, u32[]{:S(2)}) collective-permute-start(f32[192,768]{1,0:T(8,128)S(1)} %get-tuple-element.50), channel_id=1, source_target_pairs={{6,0},{7,1},{4,2},{5,3},{2,4},{3,5},{0,6},{1,7},{14,8},{15,9},{12,... | collective-permute-start | bytes 1769480 | tf_op jit(solution)/shard_map/ppermute | solution.py:270
  114.6 36.9 %collective-permute-start.10 = (f32[3,192,768]{2,1,0:T(8,128)}, f32[3,192,768]{2,1,0:T(8,128)S(1)}, u32[]{:S(2)}, u32[]{:S(2)}) collective-permute-start(f32[3,192,768]{2,1,0:T(8,128)} %get-tuple-element.55), channel_id=1, source_target_pairs={{0,8},{8,0},{16,24},{24,16},{1,9},{9,1},{17,25},{25,17},{2,10},{10... | collective-permute-start | bytes 5308424 | tf_op jit(solution)/shard_map/ppermute | solution.py:304
  116.1 36.6 %collective-permute-start.13 = (f32[3,192,768]{2,1,0:T(8,128)}, f32[3,192,768]{2,1,0:T(8,128)S(1)}, u32[]{:S(2)}, u32[]{:S(2)}) collective-permute-start(f32[3,192,768]{2,1,0:T(8,128)} %get-tuple-element.59), channel_id=1, source_target_pairs={{0,16},{8,24},{16,0},{24,8},{1,17},{9,25},{17,1},{25,9},{2,18},{10... | collective-permute-start | bytes 5308424 | tf_op jit(solution)/shard_map/ppermute | solution.py:304
  125.1 51.2 %collective-permute-start.3 = (f32[2,192,768]{2,1,0:T(8,128)}, f32[2,192,768]{2,1,0:T(8,128)}, u32[]{:S(2)}, u32[]{:S(2)}) collective-permute-start(f32[2,192,768]{2,1,0:T(8,128)} %get-tuple-element.51), channel_id=1, source_target_pairs={{4,0},{5,1},{6,2},{7,3},{0,4},{1,5},{2,6},{3,7},{12,8},{13,9},{14,... | collective-permute-start | bytes 3538952 | tf_op jit(solution)/shard_map/ppermute | solution.py:270
  177.9 40.6 %collective-permute-start.15 = (f32[3,192,768]{2,1,0:T(8,128)S(1)}, f32[3,192,768]{2,1,0:T(8,128)S(1)}, u32[]{:S(2)}, u32[]{:S(2)}) collective-permute-start(f32[3,192,768]{2,1,0:T(8,128)S(1)} %get-tuple-element.63), channel_id=1, source_target_pairs={{0,8},{8,0},{16,24},{24,16},{1,9},{9,1},{17,25},{25,17},{2,10},{10... | collective-permute-start | bytes 5308424 | tf_op jit(solution)/shard_map/ppermute | solution.py:304
  179.4 40.2 %collective-permute-start.11 = (f32[3,192,768]{2,1,0:T(8,128)S(1)}, f32[3,192,768]{2,1,0:T(8,128)S(1)}, u32[]{:S(2)}, u32[]{:S(2)}) collective-permute-start(f32[3,192,768]{2,1,0:T(8,128)S(1)} %get-tuple-element.58), channel_id=1, source_target_pairs={{0,16},{8,24},{16,0},{24,8},{1,17},{9,25},{17,1},{25,9},{2,18},{10... | collective-permute-start | bytes 5308424 | tf_op jit(solution)/shard_map/ppermute | solution.py:304
  180.9 16.6 %collective-permute-start.17 = (f32[192,768]{1,0:T(8,128)S(1)}, f32[192,768]{1,0:T(8,128)S(1)}, u32[]{:S(2)}, u32[]{:S(2)}) collective-permute-start(f32[192,768]{1,0:T(8,128)S(1)} %copy-done.27), channel_id=1, source_target_pairs={{6,0},{7,1},{4,2},{5,3},{2,4},{3,5},{0,6},{1,7},{14,8},{15,9},{12,... | collective-permute-start | bytes 1769480 | tf_op jit(solution)/shard_map/ppermute | solution.py:270
  198.7 48.8 %collective-permute-start.22 = (f32[384,768]{1,0:T(8,128)S(1)}, f32[384,768]{1,0:T(8,128)S(1)}, u32[]{:S(2)}, u32[]{:S(2)}) collective-permute-start(f32[384,768]{1,0:T(8,128)S(1)} %pad_maximum_fusion.4.refs_2_), channel_id=1, source_target_pairs={{0,1},{1,0},{2,3},{3,2},{4,5},{5,4},{6,7},{7,6},{8,9},{9,8},{10,11... | collective-permute-start | bytes 3538952 | tf_op jit(solution)/shard_map/ppermute | solution.py:273
  201.5 65.4 %collective-permute-start.18 = (f32[384,768]{1,0:T(8,128)S(1)}, f32[384,768]{1,0:T(8,128)S(1)}, u32[]{:S(2)}, u32[]{:S(2)}) collective-permute-start(f32[384,768]{1,0:T(8,128)S(1)} %get-tuple-element.68), channel_id=1, source_target_pairs={{6,0},{7,1},{4,2},{5,3},{2,4},{3,5},{0,6},{1,7},{14,8},{15,9},{12,... | collective-permute-start | bytes 3538952 | tf_op jit(solution)/shard_map/ppermute | solution.py:270
  266.9 28.6 %collective-permute-start.23 = (f32[384,768]{1,0:T(8,128)S(1)}, f32[384,768]{1,0:T(8,128)S(1)}, u32[]{:S(2)}, u32[]{:S(2)}) collective-permute-start(f32[384,768]{1,0:T(8,128)S(1)} %collective-permute-done.18.refs_2_), channel_id=1, source_target_pairs={{0,1},{1,0},{2,3},{3,2},{4,5},{5,4},{6,7},{7,6},{8,9},{9,8},{10,11... | collective-permute-start | bytes 3538952 | tf_op jit(solution)/shard_map/ppermute | solution.py:273
  267.0 47.9 %collective-permute-start.19 = (f32[384,768]{1,0:T(8,128)S(1)}, f32[384,768]{1,0:T(8,128)S(1)}, u32[]{:S(2)}, u32[]{:S(2)}) collective-permute-start(f32[384,768]{1,0:T(8,128)S(1)} %get-tuple-element.69), channel_id=1, source_target_pairs={{6,0},{7,1},{4,2},{5,3},{2,4},{3,5},{0,6},{1,7},{14,8},{15,9},{12,... | collective-permute-start | bytes 3538952 | tf_op jit(solution)/shard_map/ppermute | solution.py:270
  268.6 55.1 %collective-permute-start.24 = (f32[384,768]{1,0:T(8,128)}, f32[384,768]{1,0:T(8,128)S(1)}, u32[]{:S(2)}, u32[]{:S(2)}) collective-permute-start(f32[384,768]{1,0:T(8,128)} %get-tuple-element.82), channel_id=1, source_target_pairs={{2,0},{3,1},{0,2},{1,3},{6,4},{7,5},{4,6},{5,7},{10,8},{11,9},{8,1... | collective-permute-start | bytes 3538952 | tf_op jit(solution)/shard_map/ppermute | solution.py:270
  315.0 35.0 %collective-permute-start.20 = (f32[384,768]{1,0:T(8,128)S(1)}, f32[384,768]{1,0:T(8,128)S(1)}, u32[]{:S(2)}, u32[]{:S(2)}) collective-permute-start(f32[384,768]{1,0:T(8,128)S(1)} %get-tuple-element.70), channel_id=1, source_target_pairs={{6,0},{7,1},{4,2},{5,3},{2,4},{3,5},{0,6},{1,7},{14,8},{15,9},{12,... | collective-permute-start | bytes 3538952 | tf_op jit(solution)/shard_map/ppermute | solution.py:270
  317.4 57.7 %collective-permute-start.26 = (f32[384,768]{1,0:T(8,128)}, f32[384,768]{1,0:T(8,128)S(1)}, u32[]{:S(2)}, u32[]{:S(2)}) collective-permute-start(f32[384,768]{1,0:T(8,128)} %get-tuple-element.86), channel_id=1, source_target_pairs={{2,0},{3,1},{0,2},{1,3},{6,4},{7,5},{4,6},{5,7},{10,8},{11,9},{8,1... | collective-permute-start | bytes 3538952 | tf_op jit(solution)/shard_map/ppermute | solution.py:270
  350.0 25.1 %collective-permute-start.27 = (f32[384,768]{1,0:T(8,128)S(1)}, f32[384,768]{1,0:T(8,128)S(1)}, u32[]{:S(2)}, u32[]{:S(2)}) collective-permute-start(f32[384,768]{1,0:T(8,128)S(1)} %collective-permute-done.20.refs_2_), channel_id=1, source_target_pairs={{0,1},{1,0},{2,3},{3,2},{4,5},{5,4},{6,7},{7,6},{8,9},{9,8},{10,11... | collective-permute-start | bytes 3538952 | tf_op jit(solution)/shard_map/ppermute | solution.py:273
  350.0 52.1 %collective-permute-start.29 = (f32[384,768]{1,0:T(8,128)}, f32[384,768]{1,0:T(8,128)S(1)}, u32[]{:S(2)}, u32[]{:S(2)}) collective-permute-start(f32[384,768]{1,0:T(8,128)} %get-tuple-element.90), channel_id=1, source_target_pairs={{2,0},{3,1},{0,2},{1,3},{6,4},{7,5},{4,6},{5,7},{10,8},{11,9},{8,1... | collective-permute-start | bytes 3538952 | tf_op jit(solution)/shard_map/ppermute | solution.py:270
  394.4 32.8 %collective-permute-start.28 = (f32[384,768]{1,0:T(8,128)}, f32[384,768]{1,0:T(8,128)S(1)}, u32[]{:S(2)}, u32[]{:S(2)}) collective-permute-start(f32[384,768]{1,0:T(8,128)} %get-tuple-element.89), channel_id=1, source_target_pairs={{2,0},{3,1},{0,2},{1,3},{6,4},{7,5},{4,6},{5,7},{10,8},{11,9},{8,1... | collective-permute-start | bytes 3538952 | tf_op jit(solution)/shard_map/ppermute | solution.py:270
  (34 other events, 252.2 us)
